TPU v7x, 32 devices: a whole 2x2x4 slice. The times are simulated.
32 devices in a mesh: chan: 16 (over z, x, core), tm: 2 (over y).
Axes of the slice: x: 2, y: 2, z: 4, core: 2. Of those that a mesh axis runs over, the one named last changes fastest.
Arguments:
- voltages: int32 [2, 64, 262144], P(None, 'chan', 'tm'), may hold values from -8 to 7
Outputs:
- visibilities: float32 [2, 1024, 64, 64], P(None, 'chan', 'tm')
Inputs may be any that keep to these rules, and one draw needn't show every extreme that they name: `voltages`: 4-bit two's complement samples.
All inputs are finite; a program needn't handle non-finite values.
Results may differ from a plain program's by a relative error of at most 0.001.
Values may be sent and summed in bfloat16 or wider, within the bound.
A program may use at most 128 MiB of HBM per device.

v0:
```python
import jax
import jax.numpy as jnp
from jax import lax
from jax.sharding import PartitionSpec as P

NCH = 1024
TAPS = 4


def passed_along(x, axis, by):
    length = lax.axis_size(axis)
    pairs = [(i, i + by) for i in range(length) if 0 <= i + by < length]
    return lax.ppermute(x, axis, pairs)


def make_taps(nch):
    k = jnp.arange(TAPS * nch, dtype=jnp.float32)
    x = (k - 2.0 * nch + 0.5) / nch
    window = 0.54 - 0.46 * jnp.cos(2.0 * jnp.pi * (k + 0.5) / (TAPS * nch))
    return (jnp.sinc(x) * window).reshape(TAPS, nch)


def turn_tables(rows, columns, period):
    left_index = jnp.arange(rows, dtype=jnp.int32)
    right_index = jnp.arange(columns, dtype=jnp.int32)
    product = left_index[:, None] * right_index[None, :] % period
    angle = product.astype(jnp.float32) * (2.0 * jnp.pi / period)
    return (jnp.cos(angle), jnp.sin(angle))


def small_dft(real_in, imag_in, spec, cosine, sine):
    high = lax.Precision.HIGHEST
    real_out = jnp.einsum(spec, real_in, cosine, precision=high) + jnp.einsum(
        spec, imag_in, sine, precision=high
    )
    imag_out = jnp.einsum(spec, imag_in, cosine, precision=high) - jnp.einsum(
        spec, real_in, sine, precision=high
    )
    return (real_out, imag_out)


def channelize(filtered, nch):
    n_first = max((d for d in range(1, nch + 1) if nch % d == 0 and d * d <= nch))
    n_second = nch // n_first
    local_inputs = filtered.shape[1]
    spec_count = filtered.shape[2]
    real_in = filtered[0].reshape(local_inputs, spec_count, n_first, n_second)
    imag_in = filtered[1].reshape(local_inputs, spec_count, n_first, n_second)
    cos_first, sin_first = turn_tables(n_first, n_first, n_first)
    real_mid, imag_mid = small_dft(real_in, imag_in, "asmn,mk->askn", cos_first, sin_first)
    cos_twiddle, sin_twiddle = turn_tables(n_first, n_second, nch)
    twist_real = real_mid * cos_twiddle + imag_mid * sin_twiddle
    twist_imag = imag_mid * cos_twiddle - real_mid * sin_twiddle
    cos_second, sin_second = turn_tables(n_second, n_second, n_second)
    real_out, imag_out = small_dft(twist_real, twist_imag, "askn,nj->jkas", cos_second, sin_second)
    norm = 1.0 / jnp.sqrt(jnp.float32(nch))
    real_out = real_out.reshape(nch, local_inputs, spec_count) * norm
    imag_out = imag_out.reshape(nch, local_inputs, spec_count) * norm
    return jnp.stack([real_out, imag_out], axis=1)


def correlate(rows, columns):
    rows_real = rows[:, 0]
    rows_imag = rows[:, 1]
    left = jnp.stack(
        [
            jnp.concatenate([rows_real, rows_imag], axis=-1),
            jnp.concatenate([rows_imag, -rows_real], axis=-1),
        ],
        axis=1,
    )
    right = jnp.concatenate([columns[:, 0], columns[:, 1]], axis=-1)
    return jnp.einsum("cqak,cbk->qcab", left, right, preferred_element_type=jnp.float32)


def local(voltages):
    nch = NCH
    local_inputs = voltages.shape[1]
    spec_count = voltages.shape[2] // nch
    raw = voltages.reshape(2, local_inputs, spec_count, nch)
    tail = raw[:, :, spec_count - (TAPS - 1) :, :]
    earlier = passed_along(tail, "tm", 1)
    combined = jnp.concatenate([earlier, raw], axis=2).astype(jnp.float32) * 0.25
    taps = make_taps(nch)
    filtered = taps[0] * combined[:, :, 0:spec_count, :]
    for step in range(1, TAPS):
        filtered = filtered + taps[step] * combined[:, :, step : step + spec_count, :]
    spectra = channelize(filtered, nch).astype(jnp.bfloat16)
    owned = lax.all_to_all(spectra, "chan", split_axis=0, concat_axis=2, tiled=True)
    blocks = lax.axis_size("tm")
    scale = 1.0 / (spec_count * blocks)
    whole = lax.all_gather(owned, "tm", axis=3, tiled=True)
    half_rows = whole.shape[2] // blocks
    mine = lax.dynamic_slice_in_dim(whole, lax.axis_index("tm") * half_rows, half_rows, 2)
    return correlate(mine, whole) * scale


def solution(mesh):
    placed = (P(None, "chan", "tm"),)
    return jax.shard_map(
        local, mesh=mesh, in_specs=placed, out_specs=P(None, "chan", "tm", None), check_vma=False
    )
```

profile of v0, /device:TPU:0, one launch (start us, length us, event | category | flops | bytes accessed | tf_op | source)
XLA Modules:
  0.0 195.1 jit_solution(4726806187517959655)
XLA Ops:
  6.5 0.0 all-gather.2.cloned.1.call-start
  6.5 5.8 %reshape.80 = s32[2,4,128,1024]{3,2,1,0:T(8,128)} reshape(s32[2,4,131072]{2,1,0:T(4,128)} %param.1) | data formatting | bytes 8388608 | tf_op jit(solution)/shard_map/reshape | solution.py:80
  12.3 1.0 slice.65
  13.3 4.9 %collective-permute-start = (s32[2,4,3,1024]{3,2,1,0:T(4,128)S(1)}, s32[2,4,3,1024]{3,2,1,0:T(4,128)S(1)}, u32[]{:S(2)}, u32[]{:S(2)}) collective-permute-start(s32[2,4,3,1024]{3,2,1,0:T(4,128)S(1)} %slice.65), channel_id=1, source_target_pairs={{0,1},{2,3},{4,5},{6,7},{8,9},{10,11},{12,13},{14,15},{16,17},{18,... | collective-permute-start | bytes 294920 | tf_op jit(solution)/shard_map/ppermute | solution.py:13
  18.2 0.1 fusion.48
  18.3 0.1 fusion.92
  18.4 2.5 %collective-permute-done = s32[2,4,3,1024]{3,2,1,0:T(4,128)S(1)} collective-permute-done((s32[2,4,3,1024]{3,2,1,0:T(4,128)S(1)}, s32[2,4,3,1024]{3,2,1,0:T(4,128)S(1)}, u32[]{:S(2)}, u32[]{:S(2)}) %collective-permute-start) | collective-permute-done | bytes 98336 | tf_op jit(solution)/shard_map/ppermute | solution.py:13
  20.9 2.8 %fusion = f32[2,4,131,1024]{3,2,1,0:T(8,128)S(1)} fusion(s32[2,4,128,1024]{3,2,1,0:T(8,128)} %reshape.80, s32[2,4,3,1024]{3,2,1,0:T(4,128)S(1)} %collective-permute-done), kind=kLoop, calls=%fused_computation.1 | loop fusion | flops 3219456 | bytes 8585216 | tf_op jit(solution)/shard_map/mul | solution.py:83
  23.8 1.8 fusion.1
  25.6 2.5 %fusion.138 = (f32[1,4,128,1024]{3,2,1,0:T(8,128)}, f32[1,4,128,1024]{3,2,1,0:T(8,128)}) fusion(f32[2,4,128,1024]{3,2,1,0:T(8,128)S(1)} %fusion.1), kind=kLoop, calls=%fused_computation.148 | loop fusion | bytes 8388608 | tf_op jit(solution)/shard_map/slice | solution.py:47
  28.1 1.9 copy.38
  30.1 4.3 %fusion.18 = f32[32,4,128,32]{2,0,3,1:T(8,128)} fusion(f32[4,128,32,32]{1,3,2,0:T(8,128)S(1)} %bitcast.66), kind=kOutput, calls=%fused_computation.34 | convolution fusion | flops 201340928 | bytes 4194304 | tf_op jit(solution)/shard_map/asmn,mk->askn/dot_general | solution.py:36
  34.4 4.3 %fusion.20 = f32[32,4,128,32]{2,0,3,1:T(8,128)} fusion(f32[4,128,32,32]{1,3,2,0:T(8,128)S(1)} %bitcast.67), kind=kOutput, calls=%fused_computation.36 | convolution fusion | flops 201340928 | bytes 4194304 | tf_op jit(solution)/shard_map/asmn,mk->askn/dot_general | solution.py:33
  38.7 2.1 %copy.36 = f32[1,4,128,1024]{2,3,1,0:T(8,128)S(1)} copy(f32[1,4,128,1024]{3,2,1,0:T(8,128)} %get-tuple-element.11) | data formatting | bytes 4194304 | tf_op jit(solution)/shard_map/slice | solution.py:47
  40.8 0.0 copy-start.1
  40.8 4.8 %fusion.26 = f32[32,4,128,32]{2,0,3,1:T(8,128)S(1)} fusion(f32[32,4,128,32]{2,0,3,1:T(8,128)} %fusion.20, f32[4,128,32,32]{1,3,2,0:T(8,128)S(1)} %bitcast.64), kind=kOutput, calls=%fused_computation.42 | convolution fusion | flops 201865216 | bytes 6291456 | tf_op jit(solution)/shard_map/asmn,mk->askn/dot_general | solution.py:33
  45.7 0.0 copy-done.1
  45.7 3.7 %add_bitcast_fusion = (f32[4,128,32,32]{1,2,3,0:T(8,128)S(1)}, f32[4,128,32,32]{1,2,3,0:T(8,128)S(1)}) fusion(f32[32,4,128,32]{2,0,3,1:T(8,128)S(1)} %fusion.26, f32[32,32]{0,1:T(8,128)S(1)} %get-tuple-element.19, f32[32,32]{0,1:T(8,128)S(1)} %get-tuple-element.20, f32[32,4,128,32]{2,0,3,1:T(8,128)S(1)} %copy-done.1, f32[4,128,32,32]{1,3,2,0:T(8,128)S(1)} %bitcast.65), kind=kOutput, calls=%fused_computation.25 | convolution fusion | flops 205010944 | bytes 10493952 | tf_op jit(solution)/shard_map/asmn,mk->askn/dot_general | solution.py:36
  49.4 3.0 %fusion.10 = f32[32,4,128,32]{2,0,3,1:T(8,128)S(1)} fusion(f32[4,128,32,32]{1,2,3,0:T(8,128)S(1)} %get-tuple-element.8), kind=kOutput, calls=%fused_computation.26 | convolution fusion | flops 201340928 | bytes 4194304 | tf_op jit(solution)/shard_map/askn,nj->jkas/dot_general | solution.py:36
  52.4 3.3 %fusion.12 = f32[32,4,128,32]{2,0,3,1:T(8,128)S(1)} fusion(f32[4,128,32,32]{1,2,3,0:T(8,128)S(1)} %get-tuple-element.8), kind=kOutput, calls=%fused_computation.28 | convolution fusion | flops 201340928 | bytes 4194304 | tf_op jit(solution)/shard_map/askn,nj->jkas/dot_general | solution.py:33
  55.7 3.2 %fusion.39 = bf16[32,32,4,128]{3,0,1,2:T(8,128)(2,1)S(1)} fusion(f32[32,4,128,32]{2,0,3,1:T(8,128)S(1)} %fusion.10, f32[4,128,32,32]{1,2,3,0:T(8,128)S(1)} %get-tuple-element.7), kind=kOutput, calls=%fused_computation.45 | convolution fusion | flops 202913792 | bytes 5242880 | tf_op jit(solution)/shard_map/askn,nj->jkas/dot_general | solution.py:36
  58.9 0.4 copy.47
  59.3 3.2 %fusion.36 = bf16[32,32,4,128]{3,0,1,2:T(8,128)(2,1)S(1)} fusion(f32[32,4,128,32]{2,0,3,1:T(8,128)S(1)} %fusion.12, f32[4,128,32,32]{1,2,3,0:T(8,128)S(1)} %get-tuple-element.7), kind=kOutput, calls=%fused_computation.44 | convolution fusion | flops 202913792 | bytes 5242880 | tf_op jit(solution)/shard_map/askn,nj->jkas/dot_general | solution.py:33
  62.5 0.4 copy.44
  62.9 0.2 pad_maximum_fusion
  63.1 1.6 copy.48
  64.7 53.0 %all_to_all.18 = bf16[1024,2,4,128]{3,2,1,0:T(4,128)(2,1)S(1)} all-to-all(bf16[1024,2,4,128]{3,2,1,0:T(4,128)(2,1)S(1)} %copy.48), channel_id=1, replica_groups=mesh['chan'=16,'tm'=2] {'chan'}, dimensions={0} | all-to-all | bytes 4194304 | tf_op jit(solution)/shard_map/all_to_all | solution.py:89
  117.7 0.3 copy.49
  118.0 2.9 %copy.50 = bf16[64,2,16,4,128]{4,3,2,0,1:T(4,128)(2,1)} copy(bf16[64,2,16,4,128]{4,0,2,3,1:T(8,128)(2,1)S(1)} %bitcast.69) | data formatting | bytes 4194304 | tf_op jit(solution)/shard_map/all_to_all | solution.py:89
  121.0 0.0 all-gather.2.cloned.1.call-update
  121.0 58.3 %all-gather.2.cloned.1.call-done = bf16[64,2,64,256]{3,2,0,1:T(8,128)(2,1)} async-done(((bf16[64,2,64,128]{3,2,0,1:T(8,128)(2,1)}), bf16[64,2,64,256]{3,2,0,1:T(8,128)(2,1)}) %all-gather.2.cloned.1.call-update) | async-done | bytes 4194320 | tf_op jit(solution)/shard_map/all_gather | solution.py:92
  179.3 1.6 fusion.137
  180.9 1.3 dynamic-slice_bitcast_fusion
  182.2 0.0 copy-start
  182.2 0.4 maximum_bitcast_fusion.2
  182.7 1.8 copy-done
  184.4 0.6 slice_bitcast_fusion.1
  185.0 1.7 multiply_bitcast_fusion
  186.8 1.5 copy.52
  (1 shorter events, 0.0 us)
Async XLA Ops:
  6.5 172.7 %all-gather.2.cloned.1.call-start = ((), (), s32[]{:S(2)}) async-start(), calls=%async_computation.1 | async-start | bytes 6291456 | tf_op jit(solution)/shard_map/all_gather | solution.py:92
  13.3 7.6 %collective-permute-start = (s32[2,4,3,1024]{3,2,1,0:T(4,128)S(1)}, s32[2,4,3,1024]{3,2,1,0:T(4,128)S(1)}, u32[]{:S(2)}, u32[]{:S(2)}) collective-permute-start(s32[2,4,3,1024]{3,2,1,0:T(4,128)S(1)} %slice.65), channel_id=1, source_target_pairs={{0,1},{2,3},{4,5},{6,7},{8,9},{10,11},{12,13},{14,15},{16,17},{18,... | collective-permute-start | bytes 294920 | tf_op jit(solution)/shard_map/ppermute | solution.py:13
  40.8 4.9 %copy-start.1 = (f32[32,4,128,32]{2,0,3,1:T(8,128)S(1)}, f32[32,4,128,32]{2,0,3,1:T(8,128)}, u32[]{:S(2)}) copy-start(f32[32,4,128,32]{2,0,3,1:T(8,128)} %fusion.18) | copy-start | bytes 6291460
  182.2 2.2 %copy-start = (bf16[64,2,64,256]{3,2,0,1:T(8,128)(2,1)S(1)}, bf16[64,2,64,256]{3,2,0,1:T(8,128)(2,1)}, u32[]{:S(2)}) copy-start(bf16[64,2,64,256]{3,2,0,1:T(8,128)(2,1)} %all-gather.2.cloned.1.call-done) | copy-start | bytes 12582916
Sparse Core Ops, SparseCore 0:
  121.1 58.1 all-gather.1
where the time goes:
time: 195 us
  waiting for transfers between devices  60.8 us (31%)
  blocking collectives  53 us (27%)
  matrix products  31.6 us (16%)
  local copies, waits for them, and re-layouts  24.1 us (12%)
  between operations  13.6 us (7%)
  other arithmetic  7.09 us (4%)
  starting transfers between devices  4.88 us (3%)
    all_gather x1, waiting for transfers between devices, local(): whole = lax.all_gather(owned, 'tm', axis=3, tiled=True)  58.3 us
    all_to_all x1, blocking collectives, local(): lax.all_to_all(spectra, 'chan', split_axis=0, concat_axis=2, tiled=True)  53 us
    dot_general x2, matrix products, small_dft(): jnp.einsum(spec, real_in, cosine, precision=high)  7.99 us
    dot_general x2, matrix products, small_dft(): jnp.einsum(spec, imag_in, sine, precision=high)  7.6 us
    dot_general x2, matrix products, small_dft(): jnp.einsum(spec, imag_in, cosine, precision=high)  7.38 us
    dot_general x2, matrix products, small_dft(): jnp.einsum(spec, real_in, sine, precision=high)  6.85 us
    reshape x1, local copies, waits for them, and re-layouts, local(): raw = voltages.reshape(2, local_inputs, spec_count, nch)  5.8 us
    ppermute x1, starting transfers between devices, passed_along(): return lax.ppermute(x, axis, pairs)  4.88 us
  transfers between devices with their start and end apart: 2, of which 2 were waited for; matrix products, arithmetic and copies ran while one was open for 0% of the time, Pallas kernels for 0%

commit v1 on v0

v1 whole, which is shorter than its diff:
```python
import functools

import jax
import jax.numpy as jnp
import ml_dtypes
import numpy as np
from jax import lax
from jax.experimental import pallas as pl
from jax.experimental.pallas import tpu as pltpu
from jax.sharding import PartitionSpec as P

NCH = 1024
TAPS = 4
RADIX = 4
GROUP = 16
NT = (((1,), (1,)), ((), ()))


def make_taps(nch):
    k = np.arange(TAPS * nch, dtype=np.float64)
    x = (k - 2.0 * nch + 0.5) / nch
    window = 0.54 - 0.46 * np.cos(2.0 * np.pi * (k + 0.5) / (TAPS * nch))
    return (np.sinc(x) * window).reshape(TAPS, nch).astype(np.float32)


def make_dft(nch):
    sub = nch // RADIX
    n = np.arange(sub)
    highs, lows = [], []
    for r in range(RADIX):
        k = RADIX * np.arange(sub) + r
        angle = (k[:, None] * n[None, :] % nch) * (2.0 * np.pi / nch)
        c, s = np.cos(angle), np.sin(angle)
        m = np.block([[c, s], [-s, c]]) * (0.25 / np.sqrt(nch))
        high = m.astype(np.float32).astype(ml_dtypes.bfloat16)
        low = (m - high.astype(np.float64)).astype(np.float32).astype(ml_dtypes.bfloat16)
        highs.append(high)
        lows.append(low)
    return np.stack(highs), np.stack(lows)


def make_permutation(local_inputs):
    size = GROUP * 4 * local_inputs
    order = np.arange(size).reshape(GROUP, 2, 2, local_inputs).transpose(1, 2, 0, 3).reshape(-1)
    perm = np.zeros((size, size), np.float32)
    perm[np.arange(size), order] = 1.0
    return perm.astype(ml_dtypes.bfloat16)


def kernel(
    n,
    raw_ref,
    halo_ref,
    taps_ref,
    high_ref,
    low_ref,
    perm_ref,
    out_ref,
    ext,
    y_high,
    y_low,
    spread,
    send,
    recv,
    part,
    other,
    send_sem,
    recv_sem,
    tm_send_sem,
    tm_recv_sem,
):
    me = lax.axis_index("chan")
    t = lax.axis_index("tm")
    inputs, specs = raw_ref.shape[1], raw_ref.shape[2]
    sub = NCH // RADIX
    rows = send.shape[2]
    pairs = rows // (4 * inputs)
    groups = n // GROUP
    total = n * inputs
    half = total // 2

    barrier = pltpu.get_barrier_semaphore()

    @pl.loop(1, n)
    def _(i):
        pl.semaphore_signal(barrier, inc=1, device_id={"chan": lax.rem(me + i, n)}, device_id_type=pl.DeviceIdType.MESH)

    pl.semaphore_signal(barrier, inc=1, device_id={"tm": 1 - t}, device_id_type=pl.DeviceIdType.MESH)

    @pl.loop(0, inputs)
    def _(a):
        at = pl.multiple_of(a * specs, specs)
        for p in range(2):
            ext[p, 0:8, :] = halo_ref[p, a].astype(jnp.float32)
            ext[p, 8 : 8 + specs, :] = raw_ref[p, a].astype(jnp.float32)
        quarters = []
        for p in range(2):
            row = []
            for q in range(RADIX):
                lanes = slice(q * sub, (q + 1) * sub)
                value = taps_ref[0:1, lanes] * ext[p, 5 : 5 + specs, lanes]
                for step in range(1, TAPS):
                    value = value + taps_ref[step : step + 1, lanes] * ext[p, 5 + step : 5 + step + specs, lanes]
                row.append(value)
            quarters.append(row)
        r, im = quarters
        er, orr, dr, gr = r[0] + r[2], r[1] + r[3], r[0] - r[2], r[1] - r[3]
        ei, oi, di, gi = im[0] + im[2], im[1] + im[3], im[0] - im[2], im[1] - im[3]
        parts = [(er + orr, ei + oi), (dr + gi, di - gr), (er - orr, ei - oi), (dr - gi, di + gr)]
        for k1 in range(RADIX):
            for p in range(2):
                value = parts[k1][p]
                high = value.astype(jnp.bfloat16)
                low = (value - high.astype(jnp.float32)).astype(jnp.bfloat16)
                y_high[k1, pl.ds(at, specs), p * sub : (p + 1) * sub] = high
                y_low[k1, pl.ds(at, specs), p * sub : (p + 1) * sub] = low

    pl.semaphore_wait(barrier, n)

    @pl.loop(0, RADIX)
    def _(k1):
        for p in range(2):
            mine = slice(p * sub, (p + 1) * sub)
            mh, ml = high_ref[k1, mine, :], low_ref[k1, mine, :]
            yh, yl = y_high[k1], y_low[k1]
            value = lax.dot_general(mh, yh, NT, preferred_element_type=jnp.float32)
            value = value + lax.dot_general(mh, yl, NT, preferred_element_type=jnp.float32)
            value = value + lax.dot_general(ml, yh, NT, preferred_element_type=jnp.float32)
            for a in range(inputs):
                spread[pl.ds(p * inputs + a, sub, 2 * inputs), :] = value[:, a * specs : (a + 1) * specs]
        send[k1] = spread[...].astype(jnp.bfloat16).reshape(n, rows, specs)
        pltpu.make_async_copy(send.at[k1, me], recv.at[k1, me], recv_sem.at[k1]).start()

        @pl.loop(1, n)
        def _(i):
            to = lax.rem(me + i, n)
            pltpu.make_async_remote_copy(
                src_ref=send.at[k1, to],
                dst_ref=recv.at[k1, me],
                send_sem=send_sem.at[k1],
                recv_sem=recv_sem.at[k1],
                device_id={"chan": to},
                device_id_type=pl.DeviceIdType.MESH,
            ).start()

    def exchange(k1):
        return pltpu.make_async_remote_copy(
            src_ref=part.at[k1, :, pl.ds(pl.multiple_of((1 - t) * half, half), half), :],
            dst_ref=other.at[k1],
            send_sem=tm_send_sem.at[k1],
            recv_sem=tm_recv_sem.at[k1],
            device_id={"tm": 1 - t},
            device_id_type=pl.DeviceIdType.MESH,
        )

    def finish(k1):
        exchange(k1).wait_recv()
        own = part[k1, :, pl.ds(pl.multiple_of(t * half, half), half), :]
        out_ref[:, k1] = (own + other[k1]) * (1.0 / (2 * specs))

    @pl.loop(0, RADIX)
    def _(k1):
        pltpu.make_async_copy(recv.at[k1], recv.at[k1], recv_sem.at[k1]).wait()

        @pl.loop(0, pairs)
        def _(j):
            at = pl.multiple_of(j * 4 * inputs, 4 * inputs)
            turned = []
            for g in range(groups):
                block = recv[k1, g * GROUP : (g + 1) * GROUP, pl.ds(at, 4 * inputs), :].reshape(GROUP * 4 * inputs, specs)
                turned.append(jnp.dot(perm_ref[...], block, preferred_element_type=jnp.float32).astype(jnp.bfloat16))
            run = GROUP * inputs
            for c in range(2):
                real = jnp.concatenate([x[2 * c * run : (2 * c + 1) * run] for x in turned], axis=0)
                imag = jnp.concatenate([x[(2 * c + 1) * run : (2 * c + 2) * run] for x in turned], axis=0)
                left = jnp.concatenate([real, imag], axis=1)
                right = jnp.concatenate([left, jnp.concatenate([-imag, real], axis=1)], axis=0)
                part[k1, 2 * j + c] = lax.dot_general(left, right, NT, preferred_element_type=jnp.float32)

        exchange(k1).start()

        @pl.when(k1 > 0)
        def _():
            finish(k1 - 1)

    finish(RADIX - 1)

    @pl.loop(0, RADIX)
    def _(k1):
        exchange(k1).wait_send()
        pltpu.make_async_copy(send.at[k1, 0 : n - 1], send.at[k1, 0 : n - 1], send_sem.at[k1]).wait()


def local(n, voltages):
    inputs = voltages.shape[1]
    specs = voltages.shape[2] // NCH
    raw = voltages.reshape(2, inputs, specs, NCH)
    halo = lax.ppermute(raw[:, :, specs - 8 :, :], "tm", [(0, 1)])
    high, low = make_dft(NCH)
    chans = NCH // n
    per = chans // RADIX
    total = n * inputs
    rows = per * 2 * inputs
    whole = pl.BlockSpec(memory_space=pltpu.VMEM)
    out = pl.pallas_call(
        functools.partial(kernel, n),
        out_shape=jax.ShapeDtypeStruct((per, RADIX, total // 2, 2 * total), jnp.float32),
        in_specs=[whole] * 6,
        out_specs=whole,
        scratch_shapes=[
            pltpu.VMEM((2, specs + 8, NCH), jnp.float32),
            pltpu.VMEM((RADIX, inputs * specs, NCH // 2), jnp.bfloat16),
            pltpu.VMEM((RADIX, inputs * specs, NCH // 2), jnp.bfloat16),
            pltpu.VMEM((NCH // RADIX * 2 * inputs, specs), jnp.float32),
            pltpu.VMEM((RADIX, n, rows, specs), jnp.bfloat16),
            pltpu.VMEM((RADIX, n, rows, specs), jnp.bfloat16),
            pltpu.VMEM((RADIX, per, total, 2 * total), jnp.float32),
            pltpu.VMEM((RADIX, per, total // 2, 2 * total), jnp.float32),
            pltpu.SemaphoreType.DMA((RADIX,)),
            pltpu.SemaphoreType.DMA((RADIX,)),
            pltpu.SemaphoreType.DMA((RADIX,)),
            pltpu.SemaphoreType.DMA((RADIX,)),
        ],
        compiler_params=pltpu.CompilerParams(
            collective_id=0, has_side_effects=True, vmem_limit_bytes=60 * 1024 * 1024
        ),
    )(raw, halo, jnp.asarray(make_taps(NCH)), jnp.asarray(high), jnp.asarray(low), jnp.asarray(make_permutation(inputs)))
    out = out.reshape(chans, total // 2, 2, total)
    return jnp.transpose(out, (2, 0, 1, 3))


def solution(mesh):
    placed = (P(None, "chan", "tm"),)
    return jax.shard_map(
        functools.partial(local, mesh.shape["chan"]),
        mesh=mesh,
        in_specs=placed,
        out_specs=P(None, "chan", "tm", None),
        check_vma=False,
    )
```

time: 195 us -> 90.9 us (0.47)
  Pallas kernels: 0 us -> 67.6 us
  waiting for transfers between devices: 60.8 us -> 5.53 us
  blocking collectives: 53 us -> 0 us
  matrix products: 31.6 us -> 0 us
  between operations: 13.6 us -> 0.03 us
  local copies, waits for them, and re-layouts: 24.1 us -> 11.6 us
  other arithmetic: 7.09 us -> 0 us
    pallas_call x0 -> x1, Pallas kernels: none -> 67.6 us  [local(): pl.pallas_call(functools.partial(kernel, n), out_shape=jax.ShapeDtypeStru...]
    all_gather x1 -> x0, waiting for transfers between devices: 58.3 us -> none  [local(): whole = lax.all_gather(owned, 'tm', axis=3, tiled=True)]
    all_to_all x1 -> x0, blocking collectives: 53 us -> none  [local(): lax.all_to_all(spectra, 'chan', split_axis=0, concat_axis=2, tiled=True)]
    dot_general x9 -> x0, matrix products: 31.6 us -> none  [the longest x2 7.99 us: small_dft(): jnp.einsum(spec, real_in, cosine, precision=high)]
    slice x5 -> x1, local copies, waits for them, and re-layouts: 7.52 us -> 0.97 us  [local(): halo = lax.ppermute(raw[:, :, specs - 8:, :], 'tm', [(0, 1)])]
    reshape x1 -> x3, local copies, waits for them, and re-layouts: 5.8 us -> 9.9 us  [the longest x1 5.79 us: local(): raw = voltages.reshape(2, inputs, specs, NCH)]
    all_to_all x2 -> x0, local copies, waits for them, and re-layouts: 3.22 us -> none  [local(): lax.all_to_all(spectra, 'chan', split_axis=0, concat_axis=2, tiled=True)]
    ppermute x1, waiting for transfers between devices: 2.53 us -> 5.53 us  [local(): halo = lax.ppermute(raw[:, :, specs - 8:, :], 'tm', [(0, 1)])]
  transfers between devices with their start and end apart: 2 -> 1, of which waited for: 2 -> 1; matrix products, arithmetic and copies ran while one was open for 0% -> 0% of each run, Pallas kernels for 0% -> 0%
where the time goes in v1:
time: 90.9 us; the launch traced here: 89.6 us
  Pallas kernels  67.6 us (74%)
  local copies, waits for them, and re-layouts  11.6 us (13%)
  waiting for transfers between devices  5.53 us (6%)
  starting transfers between devices  4.89 us (5%)
    pallas_call x1, Pallas kernels, local(): pl.pallas_call(functools.partial(kernel, n), out_shape=jax.ShapeDtypeStru...  67.6 us
    reshape x1, local copies, waits for them, and re-layouts, local(): raw = voltages.reshape(2, inputs, specs, NCH)  5.79 us
    ppermute x1, waiting for transfers between devices, local(): halo = lax.ppermute(raw[:, :, specs - 8:, :], 'tm', [(0, 1)])  5.53 us
    ppermute x1, starting transfers between devices, local(): halo = lax.ppermute(raw[:, :, specs - 8:, :], 'tm', [(0, 1)])  4.89 us
    reshape x2, local copies, waits for them, and re-layouts, local(): out = out.reshape(chans, total // 2, 2, total)  4.11 us
  transfers between devices with their start and end apart: 1, of which 1 were waited for; matrix products, arithmetic and copies ran while one was open for 0% of the time, Pallas kernels for 0%

profile of v1, /device:TPU:0, one launch (start us, length us, event | category | flops | bytes accessed | tf_op | source)
XLA Modules:
  0.0 89.6 jit_solution(17483369387382356745)
XLA Ops:
  0.0 5.8 %reshape.6.raw_ref = s32[2,4,128,1024]{3,2,1,0:T(8,128)} reshape(s32[2,4,131072]{2,1,0:T(4,128)} %param.5) | data formatting | bytes 8388608 | tf_op jit(solution)/shard_map/reshape | solution.py:197
  5.8 1.0 %slice.4 = s32[2,4,8,1024]{3,2,1,0:T(8,128)S(1)} slice(s32[2,4,128,1024]{3,2,1,0:T(8,128)} %reshape.6.raw_ref), slice={[0:2], [0:4], [120:128], [0:1024]} | slice | bytes 524288 | tf_op jit(solution)/shard_map/slice | solution.py:198
  6.8 4.9 %collective-permute-start = (s32[2,4,8,1024]{3,2,1,0:T(8,128)S(1)}, s32[2,4,8,1024]{3,2,1,0:T(8,128)S(1)}, u32[]{:S(2)}, u32[]{:S(2)}) collective-permute-start(s32[2,4,8,1024]{3,2,1,0:T(8,128)S(1)} %slice.4), channel_id=1, source_target_pairs={{0,1},{2,3},{4,5},{6,7},{8,9},{10,11},{12,13},{14,15},{16,17},{18,... | collective-permute-start | bytes 786440 | tf_op jit(solution)/shard_map/ppermute | solution.py:198
  11.7 5.5 %collective-permute-done.halo_ref = s32[2,4,8,1024]{3,2,1,0:T(8,128)S(1)} collective-permute-done((s32[2,4,8,1024]{3,2,1,0:T(8,128)S(1)}, s32[2,4,8,1024]{3,2,1,0:T(8,128)S(1)}, u32[]{:S(2)}, u32[]{:S(2)}) %collective-permute-start) | collective-permute-done | bytes 262176 | tf_op jit(solution)/shard_map/ppermute | solution.py:198
  17.2 0.0 copy-start
  17.2 0.7 copy-done
  17.9 67.6 %shard_map.55 = f32[16,4,32,128]{3,2,1,0:T(8,128)} custom-call(s32[2,4,128,1024]{3,2,1,0:T(8,128)} %reshape.6.raw_ref, s32[2,4,8,1024]{3,2,1,0:T(8,128)} %copy-done, f32[4,1024]{1,0:T(4,128)} %constant.8.clone.taps_ref, bf16[4,512,512]{2,1,0:T(8,128)(2,1)} %constant.9.clone.high_ref, bf16[4,512,512]{2,1,0:T(8,128)(2,1)} %constant.10.clone.low_ref, ...), custom_call_target="tpu_custom_call" | custom-call | tf_op jit(solution)/shard_map/pallas_call | solution.py:205
  85.5 2.5 %reshape.7 = f32[64,32,2,64]{3,2,1,0:T(2,128)S(1)} reshape(f32[16,4,32,128]{3,2,1,0:T(8,128)} %shard_map.55) | data formatting | bytes 2097152 | tf_op jit(solution)/shard_map/reshape | solution.py:228
  88.0 1.6 %copy.8 = f32[64,32,2,64]{3,1,0,2:T(8,128)} copy(f32[64,32,2,64]{3,2,1,0:T(2,128)S(1)} %reshape.7) | data formatting | bytes 2097152 | tf_op jit(solution)/shard_map/reshape | solution.py:228
Async XLA Ops:
  6.8 10.4 %collective-permute-start = (s32[2,4,8,1024]{3,2,1,0:T(8,128)S(1)}, s32[2,4,8,1024]{3,2,1,0:T(8,128)S(1)}, u32[]{:S(2)}, u32[]{:S(2)}) collective-permute-start(s32[2,4,8,1024]{3,2,1,0:T(8,128)S(1)} %slice.4), channel_id=1, source_target_pairs={{0,1},{2,3},{4,5},{6,7},{8,9},{10,11},{12,13},{14,15},{16,17},{18,... | collective-permute-start | bytes 786440 | tf_op jit(solution)/shard_map/ppermute | solution.py:198
  17.2 0.7 copy-start

commit v2 on v1

v2 whole, which is shorter than its diff:
```python
import functools

import jax
import jax.numpy as jnp
import ml_dtypes
import numpy as np
from jax import lax
from jax.experimental import pallas as pl
from jax.experimental.pallas import tpu as pltpu
from jax.sharding import PartitionSpec as P

NCH = 1024
TAPS = 4
RADIX = 4
GROUP = 16
LANES = 128
BLOCK = 16
SPLIT = 2
NT = (((1,), (1,)), ((), ()))


def make_taps(nch):
    k = np.arange(TAPS * nch, dtype=np.float64)
    x = (k - 2.0 * nch + 0.5) / nch
    window = 0.54 - 0.46 * np.cos(2.0 * np.pi * (k + 0.5) / (TAPS * nch))
    return (np.sinc(x) * window).reshape(TAPS, nch).astype(np.float32)


def make_dft(nch):
    sub = nch // RADIX
    n = np.arange(sub)
    highs, lows = [], []
    for r in range(RADIX):
        k = RADIX * np.arange(sub) + r
        angle = (k[:, None] * n[None, :] % nch) * (2.0 * np.pi / nch)
        c, s = np.cos(angle), np.sin(angle)
        m = np.block([[c, s], [-s, c]]) * (0.25 / np.sqrt(nch))
        high = m.astype(np.float32).astype(ml_dtypes.bfloat16)
        low = (m - high.astype(np.float64)).astype(np.float32).astype(ml_dtypes.bfloat16)
        highs.append(high)
        lows.append(low)
    return np.stack(highs), np.stack(lows)


def make_permutation(local_inputs):
    size = GROUP * 4 * local_inputs
    order = np.arange(size).reshape(GROUP, 2, 2, local_inputs).transpose(1, 2, 0, 3).reshape(-1)
    perm = np.zeros((size, size), np.float32)
    perm[np.arange(size), order] = 1.0
    return perm.astype(ml_dtypes.bfloat16)


def kernel(
    n,
    inputs,
    specs,
    volts_ref,
    taps_ref,
    high_ref,
    low_ref,
    perm_ref,
    out_ref,
    raw,
    high,
    low,
    filtered,
    y_high,
    y_low,
    spread,
    send,
    recv,
    part,
    other,
    load_sem,
    table_sem,
    halo_send_sem,
    halo_recv_sem,
    send_sem,
    recv_sem,
    tm_send_sem,
    tm_recv_sem,
):
    me = lax.axis_index("chan")
    t = lax.axis_index("tm")
    sub = NCH // RADIX
    tiles = NCH // LANES
    frame = tiles * inputs
    before = (TAPS - 1) * frame
    chunks = recv.shape[0]
    split = chunks // RADIX
    rows = recv.shape[2]
    pairs = rows // (4 * inputs)
    groups = n // GROUP
    half = n * inputs // 2

    barrier = pltpu.get_barrier_semaphore()

    @pl.loop(1, n)
    def _(i):
        pl.semaphore_signal(barrier, inc=1, device_id={"chan": lax.rem(me + i, n)}, device_id_type=pl.DeviceIdType.MESH)

    pl.semaphore_signal(barrier, inc=1, device_id={"tm": 1 - t}, device_id_type=pl.DeviceIdType.MESH)

    loads = [
        pltpu.make_async_copy(volts_ref.at[p], raw.at[p, before : before + specs * frame, :], load_sem.at[p])
        for p in range(2)
    ]
    tables = [
        pltpu.make_async_copy(high_ref, high, table_sem.at[0]),
        pltpu.make_async_copy(low_ref, low, table_sem.at[1]),
    ]
    for copy in loads + tables:
        copy.start()

    halo = pltpu.make_async_remote_copy(
        src_ref=volts_ref.at[:, specs * frame - before : specs * frame, :],
        dst_ref=raw.at[:, 0:before, :],
        send_sem=halo_send_sem,
        recv_sem=halo_recv_sem,
        device_id={"tm": 1 - t},
        device_id_type=pl.DeviceIdType.MESH,
    )
    pl.semaphore_wait(barrier, n)

    @pl.when(t == 0)
    def _():
        halo.start()
        raw[:, 0:before, :] = jnp.zeros((2, before, LANES), jnp.int32)

    for copy in loads:
        copy.wait()

    def filter_block(b, a):
        at = b * BLOCK
        for p in range(2):
            frames = raw[p, pl.ds(at * frame + a, (BLOCK + TAPS - 1) * tiles, inputs), :].astype(jnp.float32)
            frames = frames.reshape(BLOCK + TAPS - 1, tiles, LANES)
            value = taps_ref[0] * frames[0:BLOCK]
            for step in range(1, TAPS):
                value = value + taps_ref[step] * frames[step : step + BLOCK]
            filtered[p] = value.reshape(BLOCK * tiles, LANES)
        quarter = tiles // RADIX
        place = pl.ds(pl.multiple_of(a * specs + at, BLOCK), BLOCK)
        for h in range(quarter):
            r, im = [[filtered[p, pl.ds(q * quarter + h, BLOCK, tiles), :] for q in range(RADIX)] for p in range(2)]
            er, orr, dr, gr = r[0] + r[2], r[1] + r[3], r[0] - r[2], r[1] - r[3]
            ei, oi, di, gi = im[0] + im[2], im[1] + im[3], im[0] - im[2], im[1] - im[3]
            parts = [(er + orr, ei + oi), (dr + gi, di - gr), (er - orr, ei - oi), (dr - gi, di + gr)]
            for k1 in range(RADIX):
                for p in range(2):
                    value = parts[k1][p]
                    top = value.astype(jnp.bfloat16)
                    lanes = slice(p * sub + h * LANES, p * sub + (h + 1) * LANES)
                    y_high[k1, place, lanes] = top
                    y_low[k1, place, lanes] = (value - top.astype(jnp.float32)).astype(jnp.bfloat16)

    @pl.loop(1, specs // BLOCK)
    def _(b):
        for a in range(inputs):
            filter_block(b, a)

    @pl.when(t == 1)
    def _():
        halo.wait_recv()

    for a in range(inputs):
        filter_block(0, a)

    for copy in tables:
        copy.wait()

    @pl.loop(0, RADIX)
    def _(k1):
        for p in range(2):
            mine = slice(p * sub, (p + 1) * sub)
            mh, ml = high[k1, mine, :], low[k1, mine, :]
            yh, yl = y_high[k1], y_low[k1]
            value = lax.dot_general(mh, yh, NT, preferred_element_type=jnp.float32)
            value = value + lax.dot_general(mh, yl, NT, preferred_element_type=jnp.float32)
            value = value + lax.dot_general(ml, yh, NT, preferred_element_type=jnp.float32)
            for a in range(inputs):
                spread[pl.ds(p * inputs + a, sub, 2 * inputs), :] = value[:, a * specs : (a + 1) * specs]
        send[k1] = spread[...].astype(jnp.bfloat16).reshape(n, split * rows, specs)
        for h in range(split):
            chunk = k1 * split + h
            cut = pl.ds(h * rows, rows)
            pltpu.make_async_copy(send.at[k1, me, cut], recv.at[chunk, me], recv_sem.at[chunk]).start()

            @pl.loop(0, n - 1)
            def _(i):
                step = (i + 1) // 2
                to = lax.rem(me + n + n // 2 + step * (2 * (i % 2) - 1), n)
                pltpu.make_async_remote_copy(
                    src_ref=send.at[k1, to, cut],
                    dst_ref=recv.at[chunk, me],
                    send_sem=send_sem.at[k1],
                    recv_sem=recv_sem.at[chunk],
                    device_id={"chan": to},
                    device_id_type=pl.DeviceIdType.MESH,
                ).start()

    def exchange(chunk):
        return pltpu.make_async_remote_copy(
            src_ref=part.at[chunk, :, pl.ds(pl.multiple_of((1 - t) * half, half), half), :],
            dst_ref=other.at[chunk],
            send_sem=tm_send_sem.at[chunk],
            recv_sem=tm_recv_sem.at[chunk],
            device_id={"tm": 1 - t},
            device_id_type=pl.DeviceIdType.MESH,
        )

    def finish(chunk):
        exchange(chunk).wait_recv()
        own = part[chunk, :, pl.ds(pl.multiple_of(t * half, half), half), :]
        out_ref[chunk % split, :, chunk // split] = (own + other[chunk]) * (1.0 / (2 * specs))

    @pl.loop(0, chunks)
    def _(chunk):
        pltpu.make_async_copy(recv.at[chunk], recv.at[chunk], recv_sem.at[chunk]).wait()

        @pl.loop(0, pairs)
        def _(j):
            at = pl.multiple_of(j * 4 * inputs, 4 * inputs)
            turned = []
            for g in range(groups):
                block = recv[chunk, g * GROUP : (g + 1) * GROUP, pl.ds(at, 4 * inputs), :]
                block = block.reshape(GROUP * 4 * inputs, specs)
                turned.append(jnp.dot(perm_ref[...], block, preferred_element_type=jnp.float32).astype(jnp.bfloat16))
            run = GROUP * inputs
            for c in range(2):
                real = jnp.concatenate([x[2 * c * run : (2 * c + 1) * run] for x in turned], axis=0)
                imag = jnp.concatenate([x[(2 * c + 1) * run : (2 * c + 2) * run] for x in turned], axis=0)
                left = jnp.concatenate([real, imag], axis=1)
                right = jnp.concatenate([left, jnp.concatenate([-imag, real], axis=1)], axis=0)
                part[chunk, 2 * j + c] = lax.dot_general(left, right, NT, preferred_element_type=jnp.float32)

        exchange(chunk).start()

        @pl.when(chunk > 0)
        def _():
            finish(chunk - 1)

    finish(chunks - 1)

    @pl.when(t == 0)
    def _():
        halo.wait_send()

    @pl.loop(0, chunks)
    def _(chunk):
        exchange(chunk).wait_send()

    @pl.loop(0, RADIX)
    def _(k1):
        pltpu.make_async_copy(send.at[k1, 0 : n - 1], send.at[k1, 0 : n - 1], send_sem.at[k1]).wait()


def local(n, voltages):
    inputs = voltages.shape[1]
    specs = voltages.shape[2] // NCH
    tiles = NCH // LANES
    frame = tiles * inputs
    volts = voltages.reshape(2, inputs, specs * tiles, LANES).transpose(0, 2, 1, 3).reshape(2, specs * frame, LANES)
    high, low = make_dft(NCH)
    per = NCH // n // RADIX
    split = SPLIT if per % (2 * SPLIT) == 0 else 1
    chunks, each = RADIX * split, per // split
    total = n * inputs
    rows = each * 2 * inputs
    whole = pl.BlockSpec(memory_space=pltpu.VMEM)
    there = pl.BlockSpec(memory_space=pl.ANY)
    out = pl.pallas_call(
        functools.partial(kernel, n, inputs, specs),
        out_shape=jax.ShapeDtypeStruct((split, each, RADIX, total // 2, 2 * total), jnp.float32),
        in_specs=[there, whole, there, there, whole],
        out_specs=whole,
        scratch_shapes=[
            pltpu.VMEM((2, (specs + TAPS - 1) * frame, LANES), jnp.int32),
            pltpu.VMEM((RADIX, NCH // 2, NCH // 2), jnp.bfloat16),
            pltpu.VMEM((RADIX, NCH // 2, NCH // 2), jnp.bfloat16),
            pltpu.VMEM((2, BLOCK * tiles, LANES), jnp.float32),
            pltpu.VMEM((RADIX, inputs * specs, NCH // 2), jnp.bfloat16),
            pltpu.VMEM((RADIX, inputs * specs, NCH // 2), jnp.bfloat16),
            pltpu.VMEM((NCH // RADIX * 2 * inputs, specs), jnp.float32),
            pltpu.VMEM((RADIX, n, split * rows, specs), jnp.bfloat16),
            pltpu.VMEM((chunks, n, rows, specs), jnp.bfloat16),
            pltpu.VMEM((chunks, each, total, 2 * total), jnp.float32),
            pltpu.VMEM((chunks, each, total // 2, 2 * total), jnp.float32),
            pltpu.SemaphoreType.DMA((2,)),
            pltpu.SemaphoreType.DMA((2,)),
            pltpu.SemaphoreType.DMA,
            pltpu.SemaphoreType.DMA,
            pltpu.SemaphoreType.DMA((RADIX,)),
            pltpu.SemaphoreType.DMA((chunks,)),
            pltpu.SemaphoreType.DMA((chunks,)),
            pltpu.SemaphoreType.DMA((chunks,)),
        ],
        compiler_params=pltpu.CompilerParams(
            collective_id=0, has_side_effects=True, vmem_limit_bytes=60 * 1024 * 1024
        ),
    )(
        volts,
        jnp.asarray(make_taps(NCH).reshape(TAPS, tiles, LANES)),
        jnp.asarray(high),
        jnp.asarray(low),
        jnp.asarray(make_permutation(inputs)),
    )
    out = out.reshape(1, RADIX * per, total // 2, 2 * total)
    first = lax.broadcasted_iota(jnp.int32, (2, 1, 1, 1), 0) == 0
    return jnp.where(first, out[..., :total], out[..., total:])


def solution(mesh):
    placed = (P(None, "chan", "tm"),)
    return jax.shard_map(
        functools.partial(local, mesh.shape["chan"]),
        mesh=mesh,
        in_specs=placed,
        out_specs=P(None, "chan", "tm", None),
        check_vma=False,
    )
```

time: 90.9 us -> 69.1 us (0.76); the launches traced: 89.6 us -> 68.8 us
  local copies, waits for them, and re-layouts: 11.6 us -> 1.91 us
  waiting for transfers between devices: 5.53 us -> 0 us
  starting transfers between devices: 4.89 us -> 0 us
  Pallas kernels: 67.6 us -> 65.3 us
  other arithmetic: 0 us -> 1.64 us
    reshape x3 -> x0, local copies, waits for them, and re-layouts: 9.9 us -> none  [the longest x1 5.79 us: local(): raw = voltages.reshape(2, inputs, specs, NCH)]
    ppermute x1 -> x0, waiting for transfers between devices: 5.53 us -> none  [local(): halo = lax.ppermute(raw[:, :, specs - 8:, :], 'tm', [(0, 1)])]
    ppermute x1 -> x0, starting transfers between devices: 4.89 us -> none  [local(): halo = lax.ppermute(raw[:, :, specs - 8:, :], 'tm', [(0, 1)])]
    pallas_call x1, Pallas kernels: 67.6 us -> 65.3 us  [local(): pl.pallas_call(functools.partial(kernel, n, inputs, specs), out_shape=jax...]
    broadcast_in_dim x0 -> x1, local copies, waits for them, and re-layouts: none -> 1.91 us  [local(): return jnp.where(first, out[..., :total], out[..., total:])]
    select_n x0 -> x1, other arithmetic: none -> 1.63 us  [local(): return jnp.where(first, out[..., :total], out[..., total:])]
    slice x1 -> x0, local copies, waits for them, and re-layouts: 0.97 us -> none  [local(): halo = lax.ppermute(raw[:, :, specs - 8:, :], 'tm', [(0, 1)])]
  transfers between devices with their start and end apart: 1 -> 0, of which waited for: 1 -> 0; matrix products, arithmetic and copies ran while one was open for 0% -> 0% of each run, Pallas kernels for 0% -> 0%
where the time goes in v2:
time: 69.1 us; the launch traced here: 68.8 us
  Pallas kernels  65.3 us (95%)
  local copies, waits for them, and re-layouts  1.91 us (3%)
  other arithmetic  1.64 us (2%)
    pallas_call x1, Pallas kernels, local(): pl.pallas_call(functools.partial(kernel, n, inputs, specs), out_shape=jax...  65.3 us
    broadcast_in_dim x1, local copies, waits for them, and re-layouts, local(): return jnp.where(first, out[..., :total], out[..., total:])  1.91 us
    select_n x1, other arithmetic, local(): return jnp.where(first, out[..., :total], out[..., total:])  1.63 us

profile of v2, /device:TPU:0, one launch (start us, length us, event | category | flops | bytes accessed | tf_op | source)
XLA Modules:
  0.0 68.8 jit_solution(6282047385223829500)
XLA Ops:
  0.0 65.3 %shard_map.55 = f32[2,8,4,32,128]{4,3,2,1,0:T(8,128)} custom-call(s32[2,4096,128]{2,1,0:T(8,128)} %bitcast.11, f32[4,8,128]{2,1,0:T(8,128)} %constant.10.clone.taps_ref, bf16[4,512,512]{2,1,0:T(8,128)(2,1)} %constant.11.clone.high_ref, bf16[4,512,512]{2,1,0:T(8,128)(2,1)} %constant.12.clone.low_ref, bf16[256,256]{1,0:T(8,128)(2,1)} %constant.13.clone.perm_ref), custom_call_target="tpu_custom_call" | custom-call | tf_op jit(solution)/shard_map/pallas_call | solution.py:272
  65.3 1.9 %slice_bitcast_fusion.1 = (f32[64,32,64]{2,1,0:T(8,128)S(1)}, f32[64,32,64]{2,1,0:T(8,128)S(1)}) fusion(f32[1,64,32,128]{3,2,1,0:T(8,128)} %bitcast.10), kind=kLoop, calls=%fused_computation.1 | loop fusion | bytes 2097152 | tf_op jit(solution)/shard_map/jit(_where)/broadcast_in_dim | solution.py:310
  67.2 1.6 %broadcast_select_fusion = f32[2,64,32,64]{3,2,1,0:T(8,128)} fusion(f32[64,32,64]{2,1,0:T(8,128)S(1)} %get-tuple-element.6, f32[64,32,64]{2,1,0:T(8,128)S(1)} %get-tuple-element.5, pred[2]{0:T(512)(128)(4,1)S(1)} %iota_compare_fusion), kind=kLoop, calls=%fused_computation.2 | loop fusion | flops 262144 | bytes 2097154 | tf_op jit(solution)/shard_map/jit(_where)/select_n | solution.py:310
  (1 shorter events, 0.0 us)

commit v3 on v2

--- a/solution.py
+++ b/solution.py
@@ -50,7 +50,35 @@
     return perm.astype(ml_dtypes.bfloat16)
 
 
-def kernel(
+def filter_block(b, a, inputs, specs, raw, taps_ref, filtered, y_high, y_low):
+    sub = NCH // RADIX
+    tiles = NCH // LANES
+    frame = tiles * inputs
+    at = b * BLOCK
+    for p in range(2):
+        frames = raw[p, pl.ds(at * frame + a, (BLOCK + TAPS - 1) * tiles, inputs), :].astype(jnp.float32)
+        frames = frames.reshape(BLOCK + TAPS - 1, tiles, LANES)
+        value = taps_ref[0] * frames[0:BLOCK]
+        for step in range(1, TAPS):
+            value = value + taps_ref[step] * frames[step : step + BLOCK]
+        filtered[p] = value.reshape(BLOCK * tiles, LANES)
+    quarter = tiles // RADIX
+    place = pl.ds(pl.multiple_of(a * specs + at, BLOCK), BLOCK)
+    for h in range(quarter):
+        r, im = [[filtered[p, pl.ds(q * quarter + h, BLOCK, tiles), :] for q in range(RADIX)] for p in range(2)]
+        er, orr, dr, gr = r[0] + r[2], r[1] + r[3], r[0] - r[2], r[1] - r[3]
+        ei, oi, di, gi = im[0] + im[2], im[1] + im[3], im[0] - im[2], im[1] - im[3]
+        parts = [(er + orr, ei + oi), (dr + gi, di - gr), (er - orr, ei - oi), (dr - gi, di + gr)]
+        for k1 in range(RADIX):
+            for p in range(2):
+                value = parts[k1][p]
+                top = value.astype(jnp.bfloat16)
+                lanes = slice(p * sub + h * LANES, p * sub + (h + 1) * LANES)
+                y_high[k1, place, lanes] = top
+                y_low[k1, place, lanes] = (value - top.astype(jnp.float32)).astype(jnp.bfloat16)
+
+
+def kernel_few(
     n,
     inputs,
     specs,
@@ -130,41 +158,17 @@
     for copy in loads:
         copy.wait()
 
-    def filter_block(b, a):
-        at = b * BLOCK
-        for p in range(2):
-            frames = raw[p, pl.ds(at * frame + a, (BLOCK + TAPS - 1) * tiles, inputs), :].astype(jnp.float32)
-            frames = frames.reshape(BLOCK + TAPS - 1, tiles, LANES)
-            value = taps_ref[0] * frames[0:BLOCK]
-            for step in range(1, TAPS):
-                value = value + taps_ref[step] * frames[step : step + BLOCK]
-            filtered[p] = value.reshape(BLOCK * tiles, LANES)
-        quarter = tiles // RADIX
-        place = pl.ds(pl.multiple_of(a * specs + at, BLOCK), BLOCK)
-        for h in range(quarter):
-            r, im = [[filtered[p, pl.ds(q * quarter + h, BLOCK, tiles), :] for q in range(RADIX)] for p in range(2)]
-            er, orr, dr, gr = r[0] + r[2], r[1] + r[3], r[0] - r[2], r[1] - r[3]
-            ei, oi, di, gi = im[0] + im[2], im[1] + im[3], im[0] - im[2], im[1] - im[3]
-            parts = [(er + orr, ei + oi), (dr + gi, di - gr), (er - orr, ei - oi), (dr - gi, di + gr)]
-            for k1 in range(RADIX):
-                for p in range(2):
-                    value = parts[k1][p]
-                    top = value.astype(jnp.bfloat16)
-                    lanes = slice(p * sub + h * LANES, p * sub + (h + 1) * LANES)
-                    y_high[k1, place, lanes] = top
-                    y_low[k1, place, lanes] = (value - top.astype(jnp.float32)).astype(jnp.bfloat16)
-
     @pl.loop(1, specs // BLOCK)
     def _(b):
         for a in range(inputs):
-            filter_block(b, a)
+            filter_block(b, a, inputs, specs, raw, taps_ref, filtered, y_high, y_low)
 
     @pl.when(t == 1)
     def _():
         halo.wait_recv()
 
     for a in range(inputs):
-        filter_block(0, a)
+        filter_block(0, a, inputs, specs, raw, taps_ref, filtered, y_high, y_low)
 
     for copy in tables:
         copy.wait()
@@ -255,7 +259,7 @@
         pltpu.make_async_copy(send.at[k1, 0 : n - 1], send.at[k1, 0 : n - 1], send_sem.at[k1]).wait()
 
 
-def local(n, voltages):
+def local_few(n, voltages):
     inputs = voltages.shape[1]
     specs = voltages.shape[2] // NCH
     tiles = NCH // LANES
@@ -270,7 +274,7 @@
     whole = pl.BlockSpec(memory_space=pltpu.VMEM)
     there = pl.BlockSpec(memory_space=pl.ANY)
     out = pl.pallas_call(
-        functools.partial(kernel, n, inputs, specs),
+        functools.partial(kernel_few, n, inputs, specs),
         out_shape=jax.ShapeDtypeStruct((split, each, RADIX, total // 2, 2 * total), jnp.float32),
         in_specs=[there, whole, there, there, whole],
         out_specs=whole,
@@ -310,6 +314,266 @@
     return jnp.where(first, out[..., :total], out[..., total:])
 
 
+def kernel(
+    n,
+    inputs,
+    specs,
+    volts_ref,
+    taps_ref,
+    high_ref,
+    low_ref,
+    out_ref,
+    raw,
+    high,
+    low,
+    filtered,
+    y_high,
+    y_low,
+    send,
+    recv,
+    turned,
+    part,
+    other,
+    result,
+    load_sem,
+    table_sem,
+    halo_send_sem,
+    halo_recv_sem,
+    send_sem,
+    recv_sem,
+    tm_send_sem,
+    tm_recv_sem,
+    out_sem,
+):
+    me = lax.axis_index("chan")
+    t = lax.axis_index("tm")
+    sub = NCH // RADIX
+    frame = NCH // LANES * inputs
+    before = (TAPS - 1) * frame
+    split = recv.shape[3]
+    chunks = RADIX * split
+    total = n * inputs
+    half = total // 2
+
+    barrier = pltpu.get_barrier_semaphore()
+
+    @pl.loop(1, n)
+    def _(i):
+        pl.semaphore_signal(barrier, inc=1, device_id={"chan": lax.rem(me + i, n)}, device_id_type=pl.DeviceIdType.MESH)
+
+    pl.semaphore_signal(barrier, inc=1, device_id={"tm": 1 - t}, device_id_type=pl.DeviceIdType.MESH)
+
+    loads = [
+        pltpu.make_async_copy(volts_ref.at[p], raw.at[p, before : before + specs * frame, :], load_sem.at[p])
+        for p in range(2)
+    ]
+    tables = [
+        pltpu.make_async_copy(high_ref, high, table_sem.at[0]),
+        pltpu.make_async_copy(low_ref, low, table_sem.at[1]),
+    ]
+    for copy in loads + tables:
+        copy.start()
+
+    halo = pltpu.make_async_remote_copy(
+        src_ref=volts_ref.at[:, specs * frame - before : specs * frame, :],
+        dst_ref=raw.at[:, 0:before, :],
+        send_sem=halo_send_sem,
+        recv_sem=halo_recv_sem,
+        device_id={"tm": 1 - t},
+        device_id_type=pl.DeviceIdType.MESH,
+    )
+    pl.semaphore_wait(barrier, n)
+
+    @pl.when(t == 0)
+    def _():
+        halo.start()
+        raw[:, 0:before, :] = jnp.zeros((2, before, LANES), jnp.int32)
+
+    for copy in loads:
+        copy.wait()
+
+    def transform(k1, rows, columns):
+        mh, ml = high[k1, rows, :], low[k1, rows, :]
+        yh, yl = y_high[k1, columns, :], y_low[k1, columns, :]
+        value = lax.dot_general(mh, yh, NT, preferred_element_type=jnp.float32)
+        value = value + lax.dot_general(mh, yl, NT, preferred_element_type=jnp.float32)
+        return value + lax.dot_general(ml, yh, NT, preferred_element_type=jnp.float32)
+
+    def to_partners(k1, cut, sem):
+        pltpu.make_async_copy(send.at[(k1, me) + cut], recv.at[(k1, me) + cut], sem).start()
+
+        @pl.loop(0, n - 1)
+        def _(i):
+            step = (i + 1) // 2
+            to = lax.rem(me + n + n // 2 + step * (2 * (i % 2) - 1), n)
+            pltpu.make_async_remote_copy(
+                src_ref=send.at[(k1, to) + cut],
+                dst_ref=recv.at[(k1, me) + cut],
+                send_sem=send_sem.at[k1],
+                recv_sem=sem,
+                device_id={"chan": to},
+                device_id_type=pl.DeviceIdType.MESH,
+            ).start()
+
+    for pair in range(inputs // 2):
+        pick = range(2 * pair, 2 * pair + 2)
+
+        @pl.loop(1, specs // BLOCK)
+        def _(b):
+            for a in pick:
+                filter_block(b, a, inputs, specs, raw, taps_ref, filtered, y_high, y_low)
+
+        if pair == 0:
+
+            @pl.when(t == 1)
+            def _():
+                halo.wait_recv()
+
+        for a in pick:
+            filter_block(0, a, inputs, specs, raw, taps_ref, filtered, y_high, y_low)
+        if pair == 0:
+            for copy in tables:
+                copy.wait()
+        value = transform(0, slice(0, 2 * sub), slice(2 * pair * specs, 2 * (pair + 1) * specs))
+        for i, a in enumerate(pick):
+            send[0, :, a] = value[:, i * specs : (i + 1) * specs].astype(jnp.bfloat16).reshape(n, split, 16, specs)
+        to_partners(0, (slice(2 * pair, 2 * pair + 2),), recv_sem.at[0])
+
+    @pl.loop(1, RADIX)
+    def _(k1):
+        for p in range(2):
+            value = transform(k1, slice(p * sub, (p + 1) * sub), slice(0, inputs * specs))
+            for a in range(inputs):
+                mine = value[:, a * specs : (a + 1) * specs].astype(jnp.bfloat16)
+                send[k1, p * n // 2 : (p + 1) * n // 2, a] = mine.reshape(n // 2, split, 16, specs)
+        for h in range(split):
+            to_partners(k1, (slice(0, inputs), h), recv_sem.at[k1 * split + h])
+
+    def exchange(chunk):
+        return pltpu.make_async_remote_copy(
+            src_ref=part.at[chunk, :, pl.ds(pl.multiple_of((1 - t) * half, half), half), :],
+            dst_ref=other.at[chunk],
+            send_sem=tm_send_sem.at[chunk],
+            recv_sem=tm_recv_sem.at[chunk],
+            device_id={"tm": 1 - t},
+            device_id_type=pl.DeviceIdType.MESH,
+        )
+
+    def store(chunk):
+        return pltpu.make_async_copy(
+            result.at[chunk], out_ref.at[:, chunk % split, :, chunk // split], out_sem.at[chunk]
+        )
+
+    def finish(chunk):
+        exchange(chunk).wait_recv()
+        own = part[chunk, :, pl.ds(pl.multiple_of(t * half, half), half), :]
+        value = (own + other[chunk]) * (1.0 / (2 * specs))
+        result[chunk, 0] = value[:, :, :total]
+        result[chunk, 1] = value[:, :, total:]
+        store(chunk).start()
+
+    @pl.loop(0, chunks)
+    def _(chunk):
+        k1, h = chunk // split, chunk % split
+
+        @pl.when(chunk == 0)
+        def _():
+            pltpu.make_async_copy(recv.at[0], recv.at[0], recv_sem.at[0]).wait()
+
+        @pl.when(chunk >= split)
+        def _():
+            came = recv.at[k1, :, :, h]
+            pltpu.make_async_copy(came, came, recv_sem.at[chunk]).wait()
+
+        turned[...] = recv[k1, :, :, h].astype(jnp.float32).reshape(total * 16, specs)
+        for c in range(8):
+            real = turned[pl.ds(c, total, 16), :].astype(jnp.bfloat16)
+            imag = turned[pl.ds(8 + c, total, 16), :].astype(jnp.bfloat16)
+            left = jnp.concatenate([real, imag], axis=1)
+            right = jnp.concatenate([left, jnp.concatenate([-imag, real], axis=1)], axis=0)
+            part[chunk, c] = lax.dot_general(left, right, NT, preferred_element_type=jnp.float32)
+
+        exchange(chunk).start()
+
+        @pl.when(chunk > 0)
+        def _():
+            finish(chunk - 1)
+
+    finish(chunks - 1)
+
+    @pl.when(t == 0)
+    def _():
+        halo.wait_send()
+
+    @pl.loop(0, chunks)
+    def _(chunk):
+        exchange(chunk).wait_send()
+        store(chunk).wait()
+
+    @pl.loop(0, RADIX)
+    def _(k1):
+        pltpu.make_async_copy(send.at[k1, 0 : n - 1], send.at[k1, 0 : n - 1], send_sem.at[k1]).wait()
+
+
+def local(n, voltages):
+    inputs = voltages.shape[1]
+    specs = voltages.shape[2] // NCH
+    per = NCH // n // RADIX
+    if per % 8:
+        return local_few(n, voltages)
+    tiles = NCH // LANES
+    frame = tiles * inputs
+    volts = voltages.reshape(2, inputs, specs * tiles, LANES).transpose(0, 2, 1, 3).reshape(2, specs * frame, LANES)
+    high, low = make_dft(NCH)
+    split = per // 8
+    chunks = RADIX * split
+    total = n * inputs
+
+    def tiled(m):
+        return m.reshape(RADIX, 2, NCH // RADIX // 8, 8, NCH // 2).transpose(0, 2, 1, 3, 4).reshape(m.shape)
+
+    whole = pl.BlockSpec(memory_space=pltpu.VMEM)
+    there = pl.BlockSpec(memory_space=pl.ANY)
+    out = pl.pallas_call(
+        functools.partial(kernel, n, inputs, specs),
+        out_shape=jax.ShapeDtypeStruct((2, split, 8, RADIX, total // 2, total), jnp.float32),
+        in_specs=[there, whole, there, there],
+        out_specs=there,
+        scratch_shapes=[
+            pltpu.VMEM((2, (specs + TAPS - 1) * frame, LANES), jnp.int32),
+            pltpu.VMEM((RADIX, NCH // 2, NCH // 2), jnp.bfloat16),
+            pltpu.VMEM((RADIX, NCH // 2, NCH // 2), jnp.bfloat16),
+            pltpu.VMEM((2, BLOCK * tiles, LANES), jnp.float32),
+            pltpu.VMEM((RADIX, inputs * specs, NCH // 2), jnp.bfloat16),
+            pltpu.VMEM((RADIX, inputs * specs, NCH // 2), jnp.bfloat16),
+            pltpu.VMEM((RADIX, n, inputs, split, 16, specs), jnp.bfloat16),
+            pltpu.VMEM((RADIX, n, inputs, split, 16, specs), jnp.bfloat16),
+            pltpu.VMEM((total * 16, specs), jnp.float32),
+            pltpu.VMEM((chunks, 8, total, 2 * total), jnp.float32),
+            pltpu.VMEM((chunks, 8, total // 2, 2 * total), jnp.float32),
+            pltpu.VMEM((chunks, 2, 8, total // 2, total), jnp.float32),
+            pltpu.SemaphoreType.DMA((2,)),
+            pltpu.SemaphoreType.DMA((2,)),
+            pltpu.SemaphoreType.DMA,
+            pltpu.SemaphoreType.DMA,
+            pltpu.SemaphoreType.DMA((RADIX,)),
+            pltpu.SemaphoreType.DMA((chunks,)),
+            pltpu.SemaphoreType.DMA((chunks,)),
+            pltpu.SemaphoreType.DMA((chunks,)),
+            pltpu.SemaphoreType.DMA((chunks,)),
+        ],
+        compiler_params=pltpu.CompilerParams(
+            collective_id=0, has_side_effects=True, vmem_limit_bytes=60 * 1024 * 1024
+        ),
+    )(
+        volts,
+        jnp.asarray(make_taps(NCH).reshape(TAPS, tiles, LANES)),
+        jnp.asarray(tiled(high)),
+        jnp.asarray(tiled(low)),
+    )
+    return out.reshape(2, RADIX * per, total // 2, total)
+
+
 def solution(mesh):
     placed = (P(None, "chan", "tm"),)
     return jax.shard_map(

time: 69.1 us -> 66.4 us (0.961)
  Pallas kernels: 65.3 us -> 63 us
  other arithmetic: 1.64 us -> 0 us
  local copies, waits for them, and re-layouts: 1.91 us -> 3.08 us
    unnamed x0 -> x1, local copies, waits for them, and re-layouts: none -> 3.08 us
    pallas_call x1, Pallas kernels: 65.3 us -> 63 us  [local(): pl.pallas_call(functools.partial(kernel, n, inputs, specs), out_shape=jax...]
    broadcast_in_dim x1 -> x0, local copies, waits for them, and re-layouts: 1.91 us -> none  [local(): return jnp.where(first, out[..., :total], out[..., total:])]
    select_n x1 -> x0, other arithmetic: 1.63 us -> none  [local(): return jnp.where(first, out[..., :total], out[..., total:])]
where the time goes in v3:
time: 66.4 us; the launch traced here: 66.1 us
  Pallas kernels  63 us (95%)
  local copies, waits for them, and re-layouts  3.08 us (5%)
    pallas_call x1, Pallas kernels, local(): pl.pallas_call(functools.partial(kernel, n, inputs, specs), out_shape=jax...  63 us
    unnamed x1, local copies, waits for them, and re-layouts  3.08 us

profile of v3, /device:TPU:0, one launch (start us, length us, event | category | flops | bytes accessed | tf_op | source)
XLA Modules:
  0.0 66.1 jit_solution(8269794422856526716)
XLA Ops:
  0.0 63.0 %shard_map.46 = f32[2,2,8,4,32,64]{5,4,3,2,1,0:T(8,128)} custom-call(s32[2,4096,128]{2,1,0:T(8,128)} %bitcast.7, f32[4,8,128]{2,1,0:T(8,128)} %constant.6.clone.taps_ref, bf16[4,512,512]{2,1,0:T(8,128)(2,1)} %constant.7.clone.high_ref, bf16[4,512,512]{2,1,0:T(8,128)(2,1)} %constant.8.clone.low_ref), custom_call_target="tpu_custom_call" | custom-call | tf_op jit(solution)/shard_map/pallas_call | solution.py:537
  63.0 3.1 %copy.7 = f32[2,64,32,64]{3,2,1,0:T(8,128)} copy(f32[2,64,32,64]{3,2,1,0:T(8,128)} %bitcast.6) | data formatting | bytes 2097152

commit v4 on v3

--- a/solution.py
+++ b/solution.py
@@ -371,7 +371,7 @@
         pltpu.make_async_copy(high_ref, high, table_sem.at[0]),
         pltpu.make_async_copy(low_ref, low, table_sem.at[1]),
     ]
-    for copy in loads + tables:
+    for copy in loads:
         copy.start()
 
     halo = pltpu.make_async_remote_copy(
@@ -391,6 +391,8 @@
 
     for copy in loads:
         copy.wait()
+    for copy in tables:
+        copy.start()
 
     def transform(k1, rows, columns):
         mh, ml = high[k1, rows, :], low[k1, rows, :]
@@ -415,15 +417,14 @@
                 device_id_type=pl.DeviceIdType.MESH,
             ).start()
 
-    for pair in range(inputs // 2):
-        pick = range(2 * pair, 2 * pair + 2)
+    for pick in [range(0, 1), range(1, 2)] + [range(a, a + 2) for a in range(2, inputs, 2)]:
 
         @pl.loop(1, specs // BLOCK)
         def _(b):
             for a in pick:
                 filter_block(b, a, inputs, specs, raw, taps_ref, filtered, y_high, y_low)
 
-        if pair == 0:
+        if 0 in pick:
 
             @pl.when(t == 1)
             def _():
@@ -431,13 +432,13 @@
 
         for a in pick:
             filter_block(0, a, inputs, specs, raw, taps_ref, filtered, y_high, y_low)
-        if pair == 0:
+        if 0 in pick:
             for copy in tables:
                 copy.wait()
-        value = transform(0, slice(0, 2 * sub), slice(2 * pair * specs, 2 * (pair + 1) * specs))
+        value = transform(0, slice(0, 2 * sub), slice(pick.start * specs, pick.stop * specs))
         for i, a in enumerate(pick):
             send[0, :, a] = value[:, i * specs : (i + 1) * specs].astype(jnp.bfloat16).reshape(n, split, 16, specs)
-        to_partners(0, (slice(2 * pair, 2 * pair + 2),), recv_sem.at[0])
+        to_partners(0, (slice(pick.start, pick.stop),), recv_sem.at[0])
 
     @pl.loop(1, RADIX)
     def _(k1):
@@ -449,28 +450,31 @@
         for h in range(split):
             to_partners(k1, (slice(0, inputs), h), recv_sem.at[k1 * split + h])
 
-    def exchange(chunk):
+    def exchange(chunk, q):
         return pltpu.make_async_remote_copy(
-            src_ref=part.at[chunk, :, pl.ds(pl.multiple_of((1 - t) * half, half), half), :],
-            dst_ref=other.at[chunk],
-            send_sem=tm_send_sem.at[chunk],
-            recv_sem=tm_recv_sem.at[chunk],
+            src_ref=part.at[chunk, 4 * q : 4 * q + 4, pl.ds(pl.multiple_of((1 - t) * half, half), half), :],
+            dst_ref=other.at[chunk, 4 * q : 4 * q + 4],
+            send_sem=tm_send_sem.at[chunk, q],
+            recv_sem=tm_recv_sem.at[chunk, q],
             device_id={"tm": 1 - t},
             device_id_type=pl.DeviceIdType.MESH,
         )
 
-    def store(chunk):
+    def store(chunk, q):
         return pltpu.make_async_copy(
-            result.at[chunk], out_ref.at[:, chunk % split, :, chunk // split], out_sem.at[chunk]
+            result.at[chunk, :, 4 * q : 4 * q + 4],
+            out_ref.at[:, chunk % split, 4 * q : 4 * q + 4, chunk // split],
+            out_sem.at[chunk, q],
         )
 
     def finish(chunk):
-        exchange(chunk).wait_recv()
-        own = part[chunk, :, pl.ds(pl.multiple_of(t * half, half), half), :]
-        value = (own + other[chunk]) * (1.0 / (2 * specs))
-        result[chunk, 0] = value[:, :, :total]
-        result[chunk, 1] = value[:, :, total:]
-        store(chunk).start()
+        for q in range(2):
+            exchange(chunk, q).wait_recv()
+            own = part[chunk, 4 * q : 4 * q + 4, pl.ds(pl.multiple_of(t * half, half), half), :]
+            value = (own + other[chunk, 4 * q : 4 * q + 4]) * (1.0 / (2 * specs))
+            result[chunk, 0, 4 * q : 4 * q + 4] = value[:, :, :total]
+            result[chunk, 1, 4 * q : 4 * q + 4] = value[:, :, total:]
+            store(chunk, q).start()
 
     @pl.loop(0, chunks)
     def _(chunk):
@@ -492,8 +496,8 @@
             left = jnp.concatenate([real, imag], axis=1)
             right = jnp.concatenate([left, jnp.concatenate([-imag, real], axis=1)], axis=0)
             part[chunk, c] = lax.dot_general(left, right, NT, preferred_element_type=jnp.float32)
-
-        exchange(chunk).start()
+            if c % 4 == 3:
+                exchange(chunk, c // 4).start()
 
         @pl.when(chunk > 0)
         def _():
@@ -507,8 +511,9 @@
 
     @pl.loop(0, chunks)
     def _(chunk):
-        exchange(chunk).wait_send()
-        store(chunk).wait()
+        for q in range(2):
+            exchange(chunk, q).wait_send()
+            store(chunk, q).wait()
 
     @pl.loop(0, RADIX)
     def _(k1):
@@ -533,12 +538,12 @@
         return m.reshape(RADIX, 2, NCH // RADIX // 8, 8, NCH // 2).transpose(0, 2, 1, 3, 4).reshape(m.shape)
 
     whole = pl.BlockSpec(memory_space=pltpu.VMEM)
-    there = pl.BlockSpec(memory_space=pl.ANY)
+    there = pl.BlockSpec(memory_space=pltpu.HBM)
     out = pl.pallas_call(
         functools.partial(kernel, n, inputs, specs),
         out_shape=jax.ShapeDtypeStruct((2, split, 8, RADIX, total // 2, total), jnp.float32),
         in_specs=[there, whole, there, there],
-        out_specs=there,
+        out_specs=pl.BlockSpec(memory_space=pl.ANY),
         scratch_shapes=[
             pltpu.VMEM((2, (specs + TAPS - 1) * frame, LANES), jnp.int32),
             pltpu.VMEM((RADIX, NCH // 2, NCH // 2), jnp.bfloat16),
@@ -558,12 +563,12 @@
             pltpu.SemaphoreType.DMA,
             pltpu.SemaphoreType.DMA((RADIX,)),
             pltpu.SemaphoreType.DMA((chunks,)),
-            pltpu.SemaphoreType.DMA((chunks,)),
-            pltpu.SemaphoreType.DMA((chunks,)),
-            pltpu.SemaphoreType.DMA((chunks,)),
+            pltpu.SemaphoreType.DMA((chunks, 2)),
+            pltpu.SemaphoreType.DMA((chunks, 2)),
+            pltpu.SemaphoreType.DMA((chunks, 2)),
         ],
         compiler_params=pltpu.CompilerParams(
-            collective_id=0, has_side_effects=True, vmem_limit_bytes=60 * 1024 * 1024
+            collective_id=0, has_side_effects=True, vmem_limit_bytes=(44 if total <= 64 else 60) * 1024 * 1024
         ),
     )(
         volts,

time: 66.4 us -> 66.5 us (level)
  local copies, waits for them, and re-layouts: 3.08 us -> 5.22 us
  Pallas kernels: 63 us -> 61.1 us
    unnamed x1 -> x7, local copies, waits for them, and re-layouts: 3.08 us -> 5.22 us
    pallas_call x1, Pallas kernels: 63 us -> 61.1 us  [local(): pl.pallas_call(functools.partial(kernel, n, inputs, specs), out_shape=jax...]
where the time goes in v4:
time: 66.5 us; the launch traced here: 66.3 us
  Pallas kernels  61.1 us (92%)
  local copies, waits for them, and re-layouts  5.22 us (8%)
    pallas_call x1, Pallas kernels, local(): pl.pallas_call(functools.partial(kernel, n, inputs, specs), out_shape=jax...  61.1 us
    unnamed x7, local copies, waits for them, and re-layouts  5.22 us

profile of v4, /device:TPU:0, one launch (start us, length us, event | category | flops | bytes accessed | tf_op | source)
XLA Modules:
  0.0 66.3 jit_solution(1086968933827604607)
XLA Ops:
  0.0 0.0 copy-start
  0.0 1.6 %copy-done = bf16[4,512,512]{2,1,0:T(8,128)(2,1)S(1)} copy-done((bf16[4,512,512]{2,1,0:T(8,128)(2,1)S(1)}, bf16[4,512,512]{2,1,0:T(8,128)(2,1)}, u32[]{:S(2)}) %copy-start) | copy-done | bytes 2097176
  1.6 0.0 copy-start.1
  1.6 1.6 %copy-done.1 = bf16[4,512,512]{2,1,0:T(8,128)(2,1)S(1)} copy-done((bf16[4,512,512]{2,1,0:T(8,128)(2,1)S(1)}, bf16[4,512,512]{2,1,0:T(8,128)(2,1)}, u32[]{:S(2)}) %copy-start.1) | copy-done | bytes 2097176
  3.2 0.0 copy-start.2
  3.2 0.7 %copy-done.2 = f32[4,8,128]{2,1,0:T(8,128)S(1)} copy-done((f32[4,8,128]{2,1,0:T(8,128)S(1)}, f32[4,8,128]{2,1,0:T(8,128)}, u32[]{:S(2)}) %copy-start.2) | copy-done | bytes 16408
  3.9 61.1 %shard_map.46 = f32[2,2,8,4,32,64]{5,4,3,2,1,0:T(8,128)S(1)} custom-call(s32[2,4096,128]{2,1,0:T(8,128)} %bitcast.7, f32[4,8,128]{2,1,0:T(8,128)S(1)} %copy-done.2, bf16[4,512,512]{2,1,0:T(8,128)(2,1)S(1)} %copy-done.1, bf16[4,512,512]{2,1,0:T(8,128)(2,1)S(1)} %copy-done), custom_call_target="tpu_custom_call" | custom-call | tf_op jit(solution)/shard_map/pallas_call | solution.py:542
  65.0 1.3 %copy.7 = f32[2,64,32,64]{3,2,1,0:T(8,128)} copy(f32[2,64,32,64]{3,2,1,0:T(8,128)S(1)} %bitcast.6) | data formatting | bytes 2097152
Async XLA Ops:
  0.0 1.6 %copy-start = (bf16[4,512,512]{2,1,0:T(8,128)(2,1)S(1)}, bf16[4,512,512]{2,1,0:T(8,128)(2,1)}, u32[]{:S(2)}) copy-start(bf16[4,512,512]{2,1,0:T(8,128)(2,1)} %constant.8.clone.low_ref) | copy-start | bytes 6291460
  1.6 1.6 %copy-start.1 = (bf16[4,512,512]{2,1,0:T(8,128)(2,1)S(1)}, bf16[4,512,512]{2,1,0:T(8,128)(2,1)}, u32[]{:S(2)}) copy-start(bf16[4,512,512]{2,1,0:T(8,128)(2,1)} %constant.7.clone.high_ref) | copy-start | bytes 6291460
  3.2 0.7 %copy-start.2 = (f32[4,8,128]{2,1,0:T(8,128)S(1)}, f32[4,8,128]{2,1,0:T(8,128)}, u32[]{:S(2)}) copy-start(f32[4,8,128]{2,1,0:T(8,128)} %constant.6.clone.taps_ref) | copy-start | bytes 49156

commit v5 on v4

--- a/solution.py
+++ b/solution.py
@@ -16,6 +16,8 @@
 LANES = 128
 BLOCK = 16
 SPLIT = 2
+LOADS = 4
+VMEM = 50
 NT = (((1,), (1,)), ((), ()))
 
 
@@ -319,13 +321,11 @@
     inputs,
     specs,
     volts_ref,
-    taps_ref,
-    high_ref,
-    low_ref,
+    table_ref,
     out_ref,
     raw,
-    high,
-    low,
+    table,
+    taps,
     filtered,
     y_high,
     y_low,
@@ -363,16 +363,25 @@
 
     pl.semaphore_signal(barrier, inc=1, device_id={"tm": 1 - t}, device_id_type=pl.DeviceIdType.MESH)
 
+    size = 2 * RADIX * NCH // 2
+    early = pltpu.make_async_copy(table_ref.at[size:], table.at[size:], table_sem.at[0])
+    late = pltpu.make_async_copy(table_ref.at[0:size], table.at[0:size], table_sem.at[1])
+    early.start()
+    piece = specs * frame // LOADS
     loads = [
-        pltpu.make_async_copy(volts_ref.at[p], raw.at[p, before : before + specs * frame, :], load_sem.at[p])
-        for p in range(2)
+        [
+            pltpu.make_async_copy(
+                volts_ref.at[p, g * piece : (g + 1) * piece, :],
+                raw.at[p, before + g * piece : before + (g + 1) * piece, :],
+                load_sem.at[g, p],
+            )
+            for p in range(2)
+        ]
+        for g in range(LOADS)
     ]
-    tables = [
-        pltpu.make_async_copy(high_ref, high, table_sem.at[0]),
-        pltpu.make_async_copy(low_ref, low, table_sem.at[1]),
-    ]
-    for copy in loads:
-        copy.start()
+    for group in loads:
+        for copy in group:
+            copy.start()
 
     halo = pltpu.make_async_remote_copy(
         src_ref=volts_ref.at[:, specs * frame - before : specs * frame, :],
@@ -389,25 +398,26 @@
         halo.start()
         raw[:, 0:before, :] = jnp.zeros((2, before, LANES), jnp.int32)
 
-    for copy in loads:
-        copy.wait()
-    for copy in tables:
-        copy.start()
-
-    def transform(k1, rows, columns):
-        mh, ml = high[k1, rows, :], low[k1, rows, :]
+    early.wait()
+    taps[...] = sum(
+        table[size + i * TAPS * 8 : size + (i + 1) * TAPS * 8, 0:LANES].astype(jnp.float32) for i in range(3)
+    ).reshape(TAPS, 8, LANES)
+
+    def transform(k1, rows, length, columns):
+        at = pl.multiple_of(k1 * NCH + rows, 16)
+        mh, ml = table[pl.ds(at, length), :], table[pl.ds(at + NCH // 2, length), :]
         yh, yl = y_high[k1, columns, :], y_low[k1, columns, :]
         value = lax.dot_general(mh, yh, NT, preferred_element_type=jnp.float32)
         value = value + lax.dot_general(mh, yl, NT, preferred_element_type=jnp.float32)
         return value + lax.dot_general(ml, yh, NT, preferred_element_type=jnp.float32)
 
-    def to_partners(k1, cut, sem):
-        pltpu.make_async_copy(send.at[(k1, me) + cut], recv.at[(k1, me) + cut], sem).start()
-
-        @pl.loop(0, n - 1)
+    mine, place = me // (n // 2), lax.rem(me, n // 2)
+
+    def to_half(k1, cut, sem, far):
+        @pl.loop(1 - far, n // 2)
         def _(i):
-            step = (i + 1) // 2
-            to = lax.rem(me + n + n // 2 + step * (2 * (i % 2) - 1), n)
+            side = 1 - mine if far else mine
+            to = side * (n // 2) + lax.rem(place + i, n // 2)
             pltpu.make_async_remote_copy(
                 src_ref=send.at[(k1, to) + cut],
                 dst_ref=recv.at[(k1, me) + cut],
@@ -417,12 +427,25 @@
                 device_id_type=pl.DeviceIdType.MESH,
             ).start()
 
+    def to_partners(k1, cut, sem, order):
+        for far in order:
+            to_half(k1, cut, sem, far)
+        pltpu.make_async_copy(send.at[(k1, me) + cut], recv.at[(k1, me) + cut], sem).start()
+
     for pick in [range(0, 1), range(1, 2)] + [range(a, a + 2) for a in range(2, inputs, 2)]:
 
-        @pl.loop(1, specs // BLOCK)
-        def _(b):
-            for a in pick:
-                filter_block(b, a, inputs, specs, raw, taps_ref, filtered, y_high, y_low)
+        many = specs // BLOCK // LOADS
+        for g in range(LOADS):
+            if 0 in pick:
+                for copy in loads[g]:
+                    copy.wait()
+                if g == LOADS - 1:
+                    late.start()
+
+            @pl.loop(max(1, g * many), (g + 1) * many)
+            def _(b):
+                for a in pick:
+                    filter_block(b, a, inputs, specs, raw, taps, filtered, y_high, y_low)
 
         if 0 in pick:
 
@@ -431,24 +454,23 @@
                 halo.wait_recv()
 
         for a in pick:
-            filter_block(0, a, inputs, specs, raw, taps_ref, filtered, y_high, y_low)
+            filter_block(0, a, inputs, specs, raw, taps, filtered, y_high, y_low)
         if 0 in pick:
-            for copy in tables:
-                copy.wait()
-        value = transform(0, slice(0, 2 * sub), slice(pick.start * specs, pick.stop * specs))
+            late.wait()
+        value = transform(0, 0, 2 * sub, slice(pick.start * specs, pick.stop * specs))
         for i, a in enumerate(pick):
             send[0, :, a] = value[:, i * specs : (i + 1) * specs].astype(jnp.bfloat16).reshape(n, split, 16, specs)
-        to_partners(0, (slice(pick.start, pick.stop),), recv_sem.at[0])
+        to_partners(0, (slice(pick.start, pick.stop),), recv_sem.at[0], (1, 0))
 
     @pl.loop(1, RADIX)
     def _(k1):
         for p in range(2):
-            value = transform(k1, slice(p * sub, (p + 1) * sub), slice(0, inputs * specs))
+            value = transform(k1, p * sub, sub, slice(0, inputs * specs))
             for a in range(inputs):
                 mine = value[:, a * specs : (a + 1) * specs].astype(jnp.bfloat16)
                 send[k1, p * n // 2 : (p + 1) * n // 2, a] = mine.reshape(n // 2, split, 16, specs)
         for h in range(split):
-            to_partners(k1, (slice(0, inputs), h), recv_sem.at[k1 * split + h])
+            to_partners(k1, (slice(0, inputs), h), recv_sem.at[k1 * split + h], (1, 0) if h + 1 < split else (0, 1))
 
     def exchange(chunk, q):
         return pltpu.make_async_remote_copy(
@@ -530,6 +552,11 @@
     frame = tiles * inputs
     volts = voltages.reshape(2, inputs, specs * tiles, LANES).transpose(0, 2, 1, 3).reshape(2, specs * frame, LANES)
     high, low = make_dft(NCH)
+    parts, rest = [], make_taps(NCH).reshape(-1, LANES)
+    for _ in range(3):
+        parts.append(rest.astype(ml_dtypes.bfloat16))
+        rest = rest - parts[-1].astype(np.float32)
+    parts = np.pad(np.concatenate(parts), ((0, 0), (0, NCH // 2 - LANES)))
     split = per // 8
     chunks = RADIX * split
     total = n * inputs
@@ -537,17 +564,18 @@
     def tiled(m):
         return m.reshape(RADIX, 2, NCH // RADIX // 8, 8, NCH // 2).transpose(0, 2, 1, 3, 4).reshape(m.shape)
 
-    whole = pl.BlockSpec(memory_space=pltpu.VMEM)
+    table = np.stack([tiled(high), tiled(low)], axis=1).reshape(-1, NCH // 2)
+    table = np.concatenate([table, parts])
     there = pl.BlockSpec(memory_space=pltpu.HBM)
     out = pl.pallas_call(
         functools.partial(kernel, n, inputs, specs),
         out_shape=jax.ShapeDtypeStruct((2, split, 8, RADIX, total // 2, total), jnp.float32),
-        in_specs=[there, whole, there, there],
+        in_specs=[there, there],
         out_specs=pl.BlockSpec(memory_space=pl.ANY),
         scratch_shapes=[
             pltpu.VMEM((2, (specs + TAPS - 1) * frame, LANES), jnp.int32),
-            pltpu.VMEM((RADIX, NCH // 2, NCH // 2), jnp.bfloat16),
-            pltpu.VMEM((RADIX, NCH // 2, NCH // 2), jnp.bfloat16),
+            pltpu.VMEM(table.shape, jnp.bfloat16),
+            pltpu.VMEM((TAPS, tiles, LANES), jnp.float32),
             pltpu.VMEM((2, BLOCK * tiles, LANES), jnp.float32),
             pltpu.VMEM((RADIX, inputs * specs, NCH // 2), jnp.bfloat16),
             pltpu.VMEM((RADIX, inputs * specs, NCH // 2), jnp.bfloat16),
@@ -557,7 +585,7 @@
             pltpu.VMEM((chunks, 8, total, 2 * total), jnp.float32),
             pltpu.VMEM((chunks, 8, total // 2, 2 * total), jnp.float32),
             pltpu.VMEM((chunks, 2, 8, total // 2, total), jnp.float32),
-            pltpu.SemaphoreType.DMA((2,)),
+            pltpu.SemaphoreType.DMA((LOADS, 2)),
             pltpu.SemaphoreType.DMA((2,)),
             pltpu.SemaphoreType.DMA,
             pltpu.SemaphoreType.DMA,
@@ -568,14 +596,9 @@
             pltpu.SemaphoreType.DMA((chunks, 2)),
         ],
         compiler_params=pltpu.CompilerParams(
-            collective_id=0, has_side_effects=True, vmem_limit_bytes=(44 if total <= 64 else 60) * 1024 * 1024
+            collective_id=0, has_side_effects=True, vmem_limit_bytes=VMEM * 1024 * 1024
         ),
-    )(
-        volts,
-        jnp.asarray(make_taps(NCH).reshape(TAPS, tiles, LANES)),
-        jnp.asarray(tiled(high)),
-        jnp.asarray(tiled(low)),
-    )
+    )(volts, jnp.asarray(table))
     return out.reshape(2, RADIX * per, total // 2, total)
 
 

time: 66.5 us -> 64.7 us (0.973)
  local copies, waits for them, and re-layouts: 5.22 us -> 1.32 us
  Pallas kernels: 61.1 us -> 63.2 us
    unnamed x7 -> x1, local copies, waits for them, and re-layouts: 5.22 us -> 1.32 us
    pallas_call x1, Pallas kernels: 61.1 us -> 63.2 us  [local(): pl.pallas_call(functools.partial(kernel, n, inputs, specs), out_shape=jax...]
where the time goes in v5:
time: 64.7 us; the launch traced here: 64.5 us
  Pallas kernels  63.2 us (98%)
  local copies, waits for them, and re-layouts  1.32 us (2%)
    pallas_call x1, Pallas kernels, local(): pl.pallas_call(functools.partial(kernel, n, inputs, specs), out_shape=jax...  63.2 us
    unnamed x1, local copies, waits for them, and re-layouts  1.32 us

profile of v5, /device:TPU:0, one launch (start us, length us, event | category | flops | bytes accessed | tf_op | source)
XLA Modules:
  0.0 64.5 jit_solution(10504245979434390771)
XLA Ops:
  0.0 63.2 %shard_map.28 = f32[2,2,8,4,32,64]{5,4,3,2,1,0:T(8,128)S(1)} custom-call(s32[2,4096,128]{2,1,0:T(8,128)} %bitcast.7, bf16[4192,512]{1,0:T(8,128)(2,1)} %constant.2.clone.table_ref), custom_call_target="tpu_custom_call" | custom-call | tf_op jit(solution)/shard_map/pallas_call | solution.py:570
  63.2 1.3 %copy.5 = f32[2,64,32,64]{3,2,1,0:T(8,128)} copy(f32[2,64,32,64]{3,2,1,0:T(8,128)S(1)} %bitcast.6) | data formatting | bytes 2097152

commit v6 on v5

--- a/solution.py
+++ b/solution.py
@@ -350,7 +350,7 @@
     sub = NCH // RADIX
     frame = NCH // LANES * inputs
     before = (TAPS - 1) * frame
-    split = recv.shape[3]
+    split = recv.shape[2]
     chunks = RADIX * split
     total = n * inputs
     half = total // 2
@@ -459,18 +459,21 @@
             late.wait()
         value = transform(0, 0, 2 * sub, slice(pick.start * specs, pick.stop * specs))
         for i, a in enumerate(pick):
-            send[0, :, a] = value[:, i * specs : (i + 1) * specs].astype(jnp.bfloat16).reshape(n, split, 16, specs)
-        to_partners(0, (slice(pick.start, pick.stop),), recv_sem.at[0], (1, 0))
-
-    @pl.loop(1, RADIX)
-    def _(k1):
+            send[0, :, :, a] = value[:, i * specs : (i + 1) * specs].astype(jnp.bfloat16).reshape(n, split, 16, specs)
+        to_partners(0, (slice(0, split), slice(pick.start, pick.stop)), recv_sem.at[0], (1, 0))
+
+    def issue(k1):
         for p in range(2):
             value = transform(k1, p * sub, sub, slice(0, inputs * specs))
             for a in range(inputs):
                 mine = value[:, a * specs : (a + 1) * specs].astype(jnp.bfloat16)
-                send[k1, p * n // 2 : (p + 1) * n // 2, a] = mine.reshape(n // 2, split, 16, specs)
+                send[k1, p * n // 2 : (p + 1) * n // 2, :, a] = mine.reshape(n // 2, split, 16, specs)
         for h in range(split):
-            to_partners(k1, (slice(0, inputs), h), recv_sem.at[k1 * split + h], (1, 0) if h + 1 < split else (0, 1))
+            to_partners(k1, (h,), recv_sem.at[k1 * split + h], (1, 0) if h + 1 < split else (0, 1))
+
+    def sent(k1):
+        left = send.at[k1, 0 : n - 1]
+        return pltpu.make_async_copy(left, left, send_sem.at[k1])
 
     def exchange(chunk, q):
         return pltpu.make_async_remote_copy(
@@ -498,20 +501,27 @@
             result[chunk, 1, 4 * q : 4 * q + 4] = value[:, :, total:]
             store(chunk, q).start()
 
+    issue(1)
+
     @pl.loop(0, chunks)
     def _(chunk):
         k1, h = chunk // split, chunk % split
 
+        @pl.when((h == 0) & (k1 + 2 < RADIX))
+        def _():
+            sent(k1).wait()
+            issue(k1 + 2)
+
         @pl.when(chunk == 0)
         def _():
             pltpu.make_async_copy(recv.at[0], recv.at[0], recv_sem.at[0]).wait()
 
         @pl.when(chunk >= split)
         def _():
-            came = recv.at[k1, :, :, h]
+            came = recv.at[k1, :, h]
             pltpu.make_async_copy(came, came, recv_sem.at[chunk]).wait()
 
-        turned[...] = recv[k1, :, :, h].astype(jnp.float32).reshape(total * 16, specs)
+        turned[...] = recv[k1, :, h].astype(jnp.float32).reshape(total * 16, specs)
         for c in range(8):
             real = turned[pl.ds(c, total, 16), :].astype(jnp.bfloat16)
             imag = turned[pl.ds(8 + c, total, 16), :].astype(jnp.bfloat16)
@@ -537,9 +547,8 @@
             exchange(chunk, q).wait_send()
             store(chunk, q).wait()
 
-    @pl.loop(0, RADIX)
-    def _(k1):
-        pltpu.make_async_copy(send.at[k1, 0 : n - 1], send.at[k1, 0 : n - 1], send_sem.at[k1]).wait()
+    for k1 in range(RADIX - 2, RADIX):
+        sent(k1).wait()
 
 
 def local(n, voltages):
@@ -579,8 +588,8 @@
             pltpu.VMEM((2, BLOCK * tiles, LANES), jnp.float32),
             pltpu.VMEM((RADIX, inputs * specs, NCH // 2), jnp.bfloat16),
             pltpu.VMEM((RADIX, inputs * specs, NCH // 2), jnp.bfloat16),
-            pltpu.VMEM((RADIX, n, inputs, split, 16, specs), jnp.bfloat16),
-            pltpu.VMEM((RADIX, n, inputs, split, 16, specs), jnp.bfloat16),
+            pltpu.VMEM((RADIX, n, split, inputs, 16, specs), jnp.bfloat16),
+            pltpu.VMEM((RADIX, n, split, inputs, 16, specs), jnp.bfloat16),
             pltpu.VMEM((total * 16, specs), jnp.float32),
             pltpu.VMEM((chunks, 8, total, 2 * total), jnp.float32),
             pltpu.VMEM((chunks, 8, total // 2, 2 * total), jnp.float32),

time: 64.7 us -> 65 us (level)
  no operation moved by 1% of the time
where the time goes in v6:
time: 65 us; the launch traced here: 64.9 us
  Pallas kernels  63.5 us (98%)
  local copies, waits for them, and re-layouts  1.32 us (2%)
    pallas_call x1, Pallas kernels, local(): pl.pallas_call(functools.partial(kernel, n, inputs, specs), out_shape=jax...  63.5 us
    unnamed x1, local copies, waits for them, and re-layouts  1.32 us

profile of v6, /device:TPU:0, one launch (start us, length us, event | category | flops | bytes accessed | tf_op | source)
XLA Modules:
  0.0 64.9 jit_solution(7309953334933702192)
XLA Ops:
  0.0 63.5 %shard_map.28 = f32[2,2,8,4,32,64]{5,4,3,2,1,0:T(8,128)S(1)} custom-call(s32[2,4096,128]{2,1,0:T(8,128)} %bitcast.7, bf16[4192,512]{1,0:T(8,128)(2,1)} %constant.2.clone.table_ref), custom_call_target="tpu_custom_call" | custom-call | tf_op jit(solution)/shard_map/pallas_call | solution.py:579
  63.6 1.3 %copy.5 = f32[2,64,32,64]{3,2,1,0:T(8,128)} copy(f32[2,64,32,64]{3,2,1,0:T(8,128)S(1)} %bitcast.6) | data formatting | bytes 2097152

commit v7 on v6

--- a/solution.py
+++ b/solution.py
@@ -365,7 +365,11 @@
 
     size = 2 * RADIX * NCH // 2
     early = pltpu.make_async_copy(table_ref.at[size:], table.at[size:], table_sem.at[0])
-    late = pltpu.make_async_copy(table_ref.at[0:size], table.at[0:size], table_sem.at[1])
+
+    def matrices(k1):
+        rows = pl.ds(pl.multiple_of(k1 * NCH, NCH), NCH)
+        return pltpu.make_async_copy(table_ref.at[rows], table.at[rows], table_sem.at[1 + k1])
+
     early.start()
     piece = specs * frame // LOADS
     loads = [
@@ -382,6 +386,7 @@
     for group in loads:
         for copy in group:
             copy.start()
+    matrices(0).start()
 
     halo = pltpu.make_async_remote_copy(
         src_ref=volts_ref.at[:, specs * frame - before : specs * frame, :],
@@ -391,13 +396,6 @@
         device_id={"tm": 1 - t},
         device_id_type=pl.DeviceIdType.MESH,
     )
-    pl.semaphore_wait(barrier, n)
-
-    @pl.when(t == 0)
-    def _():
-        halo.start()
-        raw[:, 0:before, :] = jnp.zeros((2, before, LANES), jnp.int32)
-
     early.wait()
     taps[...] = sum(
         table[size + i * TAPS * 8 : size + (i + 1) * TAPS * 8, 0:LANES].astype(jnp.float32) for i in range(3)
@@ -432,48 +430,61 @@
             to_half(k1, cut, sem, far)
         pltpu.make_async_copy(send.at[(k1, me) + cut], recv.at[(k1, me) + cut], sem).start()
 
-    for pick in [range(0, 1), range(1, 2)] + [range(a, a + 2) for a in range(2, inputs, 2)]:
-
-        many = specs // BLOCK // LOADS
-        for g in range(LOADS):
-            if 0 in pick:
-                for copy in loads[g]:
-                    copy.wait()
-                if g == LOADS - 1:
-                    late.start()
-
-            @pl.loop(max(1, g * many), (g + 1) * many)
-            def _(b):
-                for a in pick:
-                    filter_block(b, a, inputs, specs, raw, taps, filtered, y_high, y_low)
-
+    many = specs // BLOCK // LOADS
+
+    def filter_some(first, last, a):
+        @pl.loop(first, last)
+        def _(b):
+            filter_block(b, a, inputs, specs, raw, taps, filtered, y_high, y_low)
+
+    for g in range(LOADS):
+        for copy in loads[g]:
+            copy.wait()
+        filter_some(max(1, g * many), (g + 1) * many, 0)
+    for k1 in range(1, RADIX):
+        matrices(k1).start()
+
+    pl.semaphore_wait(barrier, n)
+
+    @pl.when(t == 0)
+    def _():
+        halo.start()
+        raw[:, 0:before, :] = jnp.zeros((2, before, LANES), jnp.int32)
+
+    filter_some(1, specs // BLOCK, 1)
+
+    @pl.when(t == 1)
+    def _():
+        halo.wait_recv()
+
+    for pick in [range(a, a + 2) for a in range(0, inputs, 2)]:
+        for a in pick:
+            filter_some(0, 1 if 0 in pick else specs // BLOCK, a)
         if 0 in pick:
-
-            @pl.when(t == 1)
-            def _():
-                halo.wait_recv()
-
-        for a in pick:
-            filter_block(0, a, inputs, specs, raw, taps, filtered, y_high, y_low)
-        if 0 in pick:
-            late.wait()
+            matrices(0).wait()
         value = transform(0, 0, 2 * sub, slice(pick.start * specs, pick.stop * specs))
         for i, a in enumerate(pick):
             send[0, :, :, a] = value[:, i * specs : (i + 1) * specs].astype(jnp.bfloat16).reshape(n, split, 16, specs)
         to_partners(0, (slice(0, split), slice(pick.start, pick.stop)), recv_sem.at[0], (1, 0))
 
-    def issue(k1):
+    def fill(k1):
+        matrices(k1).wait()
         for p in range(2):
             value = transform(k1, p * sub, sub, slice(0, inputs * specs))
             for a in range(inputs):
                 mine = value[:, a * specs : (a + 1) * specs].astype(jnp.bfloat16)
                 send[k1, p * n // 2 : (p + 1) * n // 2, :, a] = mine.reshape(n // 2, split, 16, specs)
-        for h in range(split):
-            to_partners(k1, (h,), recv_sem.at[k1 * split + h], (1, 0) if h + 1 < split else (0, 1))
-
-    def sent(k1):
-        left = send.at[k1, 0 : n - 1]
-        return pltpu.make_async_copy(left, left, send_sem.at[k1])
+
+    last = RADIX - 1
+
+    @pl.loop(1, last)
+    def _(k1):
+        fill(k1)
+        to_partners(k1, (), recv_sem.at[k1 * split], (1, 0))
+
+    fill(last)
+    for h in range(split):
+        to_partners(last, (h,), recv_sem.at[last * split + h], (1, 0) if h + 1 < split else (0, 1))
 
     def exchange(chunk, q):
         return pltpu.make_async_remote_copy(
@@ -501,24 +512,17 @@
             result[chunk, 1, 4 * q : 4 * q + 4] = value[:, :, total:]
             store(chunk, q).start()
 
-    issue(1)
-
     @pl.loop(0, chunks)
     def _(chunk):
         k1, h = chunk // split, chunk % split
 
-        @pl.when((h == 0) & (k1 + 2 < RADIX))
+        @pl.when((k1 < last) & (h == 0))
         def _():
-            sent(k1).wait()
-            issue(k1 + 2)
-
-        @pl.when(chunk == 0)
+            pltpu.make_async_copy(recv.at[k1], recv.at[k1], recv_sem.at[chunk]).wait()
+
+        @pl.when(k1 == last)
         def _():
-            pltpu.make_async_copy(recv.at[0], recv.at[0], recv_sem.at[0]).wait()
-
-        @pl.when(chunk >= split)
-        def _():
-            came = recv.at[k1, :, h]
+            came = recv.at[last, :, h]
             pltpu.make_async_copy(came, came, recv_sem.at[chunk]).wait()
 
         turned[...] = recv[k1, :, h].astype(jnp.float32).reshape(total * 16, specs)
@@ -547,8 +551,9 @@
             exchange(chunk, q).wait_send()
             store(chunk, q).wait()
 
-    for k1 in range(RADIX - 2, RADIX):
-        sent(k1).wait()
+    @pl.loop(0, RADIX)
+    def _(k1):
+        pltpu.make_async_copy(send.at[k1, 0 : n - 1], send.at[k1, 0 : n - 1], send_sem.at[k1]).wait()
 
 
 def local(n, voltages):
@@ -595,7 +600,7 @@
             pltpu.VMEM((chunks, 8, total // 2, 2 * total), jnp.float32),
             pltpu.VMEM((chunks, 2, 8, total // 2, total), jnp.float32),
             pltpu.SemaphoreType.DMA((LOADS, 2)),
-            pltpu.SemaphoreType.DMA((2,)),
+            pltpu.SemaphoreType.DMA((1 + RADIX,)),
             pltpu.SemaphoreType.DMA,
             pltpu.SemaphoreType.DMA,
             pltpu.SemaphoreType.DMA((RADIX,)),

time: 65 us -> 69 us (1.062)
  Pallas kernels: 63.5 us -> 67.5 us
    pallas_call x1, Pallas kernels: 63.5 us -> 67.5 us  [local(): pl.pallas_call(functools.partial(kernel, n, inputs, specs), out_shape=jax...]
where the time goes in v7:
time: 69 us; the launch traced here: 68.9 us
  Pallas kernels  67.5 us (98%)
  local copies, waits for them, and re-layouts  1.32 us (2%)
    pallas_call x1, Pallas kernels, local(): pl.pallas_call(functools.partial(kernel, n, inputs, specs), out_shape=jax...  67.5 us

profile of v7, /device:TPU:0, one launch (start us, length us, event | category | flops | bytes accessed | tf_op | source)
XLA Modules:
  0.0 68.9 jit_solution(14875114366002627615)
XLA Ops:
  0.0 67.5 %shard_map.28 = f32[2,2,8,4,32,64]{5,4,3,2,1,0:T(8,128)S(1)} custom-call(s32[2,4096,128]{2,1,0:T(8,128)} %bitcast.7, bf16[4192,512]{1,0:T(8,128)(2,1)} %constant.2.clone.table_ref), custom_call_target="tpu_custom_call" | custom-call | tf_op jit(solution)/shard_map/pallas_call | solution.py:584
  67.5 1.3 %copy.5 = f32[2,64,32,64]{3,2,1,0:T(8,128)} copy(f32[2,64,32,64]{3,2,1,0:T(8,128)S(1)} %bitcast.6) | data formatting | bytes 2097152

commit v8 on v5

--- a/solution.py
+++ b/solution.py
@@ -365,7 +365,11 @@
 
     size = 2 * RADIX * NCH // 2
     early = pltpu.make_async_copy(table_ref.at[size:], table.at[size:], table_sem.at[0])
-    late = pltpu.make_async_copy(table_ref.at[0:size], table.at[0:size], table_sem.at[1])
+
+    def matrices(k1):
+        rows = pl.ds(pl.multiple_of(k1 * NCH, NCH), NCH)
+        return pltpu.make_async_copy(table_ref.at[rows], table.at[rows], table_sem.at[1 + k1])
+
     early.start()
     piece = specs * frame // LOADS
     loads = [
@@ -382,6 +386,7 @@
     for group in loads:
         for copy in group:
             copy.start()
+    matrices(0).start()
 
     halo = pltpu.make_async_remote_copy(
         src_ref=volts_ref.at[:, specs * frame - before : specs * frame, :],
@@ -413,11 +418,8 @@
 
     mine, place = me // (n // 2), lax.rem(me, n // 2)
 
-    def to_half(k1, cut, sem, far):
-        @pl.loop(1 - far, n // 2)
-        def _(i):
-            side = 1 - mine if far else mine
-            to = side * (n // 2) + lax.rem(place + i, n // 2)
+    def to_partners(k1, cut, sem):
+        def give(to):
             pltpu.make_async_remote_copy(
                 src_ref=send.at[(k1, to) + cut],
                 dst_ref=recv.at[(k1, me) + cut],
@@ -427,9 +429,14 @@
                 device_id_type=pl.DeviceIdType.MESH,
             ).start()
 
-    def to_partners(k1, cut, sem, order):
-        for far in order:
-            to_half(k1, cut, sem, far)
+        give((1 - mine) * (n // 2) + place)
+
+        @pl.loop(1, n // 2)
+        def _(i):
+            step = lax.rem(place + i, n // 2)
+            give(mine * (n // 2) + step)
+            give((1 - mine) * (n // 2) + step)
+
         pltpu.make_async_copy(send.at[(k1, me) + cut], recv.at[(k1, me) + cut], sem).start()
 
     for pick in [range(0, 1), range(1, 2)] + [range(a, a + 2) for a in range(2, inputs, 2)]:
@@ -440,7 +447,8 @@
                 for copy in loads[g]:
                     copy.wait()
                 if g == LOADS - 1:
-                    late.start()
+                    for k1 in range(1, RADIX):
+                        matrices(k1).start()
 
             @pl.loop(max(1, g * many), (g + 1) * many)
             def _(b):
@@ -456,21 +464,22 @@
         for a in pick:
             filter_block(0, a, inputs, specs, raw, taps, filtered, y_high, y_low)
         if 0 in pick:
-            late.wait()
+            matrices(0).wait()
         value = transform(0, 0, 2 * sub, slice(pick.start * specs, pick.stop * specs))
         for i, a in enumerate(pick):
             send[0, :, a] = value[:, i * specs : (i + 1) * specs].astype(jnp.bfloat16).reshape(n, split, 16, specs)
-        to_partners(0, (slice(pick.start, pick.stop),), recv_sem.at[0], (1, 0))
+        to_partners(0, (slice(pick.start, pick.stop),), recv_sem.at[0])
 
     @pl.loop(1, RADIX)
     def _(k1):
+        matrices(k1).wait()
         for p in range(2):
             value = transform(k1, p * sub, sub, slice(0, inputs * specs))
             for a in range(inputs):
                 mine = value[:, a * specs : (a + 1) * specs].astype(jnp.bfloat16)
                 send[k1, p * n // 2 : (p + 1) * n // 2, a] = mine.reshape(n // 2, split, 16, specs)
         for h in range(split):
-            to_partners(k1, (slice(0, inputs), h), recv_sem.at[k1 * split + h], (1, 0) if h + 1 < split else (0, 1))
+            to_partners(k1, (slice(0, inputs), h), recv_sem.at[k1 * split + h])
 
     def exchange(chunk, q):
         return pltpu.make_async_remote_copy(
@@ -586,7 +595,7 @@
             pltpu.VMEM((chunks, 8, total // 2, 2 * total), jnp.float32),
             pltpu.VMEM((chunks, 2, 8, total // 2, total), jnp.float32),
             pltpu.SemaphoreType.DMA((LOADS, 2)),
-            pltpu.SemaphoreType.DMA((2,)),
+            pltpu.SemaphoreType.DMA((1 + RADIX,)),
             pltpu.SemaphoreType.DMA,
             pltpu.SemaphoreType.DMA,
             pltpu.SemaphoreType.DMA((RADIX,)),

time: 64.7 us -> 64.2 us (level)
  no operation moved by 1% of the time
where the time goes in v8:
time: 64.2 us; the launch traced here: 64.1 us
  Pallas kernels  62.7 us (98%)
  local copies, waits for them, and re-layouts  1.32 us (2%)
    pallas_call x1, Pallas kernels, local(): pl.pallas_call(functools.partial(kernel, n, inputs, specs), out_shape=jax...  62.7 us
    unnamed x1, local copies, waits for them, and re-layouts  1.32 us

profile of v8, /device:TPU:0, one launch (start us, length us, event | category | flops | bytes accessed | tf_op | source)
XLA Modules:
  0.0 64.1 jit_solution(10822167780512399147)
XLA Ops:
  0.0 62.7 %shard_map.28 = f32[2,2,8,4,32,64]{5,4,3,2,1,0:T(8,128)S(1)} custom-call(s32[2,4096,128]{2,1,0:T(8,128)} %bitcast.7, bf16[4192,512]{1,0:T(8,128)(2,1)} %constant.2.clone.table_ref), custom_call_target="tpu_custom_call" | custom-call | tf_op jit(solution)/shard_map/pallas_call | solution.py:579
  62.8 1.3 %copy.5 = f32[2,64,32,64]{3,2,1,0:T(8,128)} copy(f32[2,64,32,64]{3,2,1,0:T(8,128)S(1)} %bitcast.6) | data formatting | bytes 2097152
